TPU v7x, 128 devices: a whole 4x4x4 slice. The times are simulated.
128 devices in a mesh: dev: 128 (over y, z, x, core).
Axes of the slice: x: 4, y: 4, z: 4, core: 2. Of those that a mesh axis runs over, the one named last changes fastest.
Arguments:
- density_rows: bfloat16 [98304, 3840], P('dev')
- center_x: float32 [98304], replicated, may hold values from -0.25 to 1.25
- center_y: float32 [98304], replicated, may hold values from 0 to 1
- center_z: float32 [98304], replicated, may hold values from 0 to 1
- exponent: float32 [98304], replicated, may hold values from 0.5 to 150
- brick_blocks: int32 [128, 8], replicated, may hold values from 0 to 767, as said below
Outputs:
- potential: float32 [128, 4096], P('dev')
- ham_rows: float32 [98304, 3840], P('dev')
Inputs may be any that keep to these rules, and one draw needn't show every extreme that they name: `brick_blocks`: brick b belongs to device d = b. Its 8 entries are distinct blocks; 4 of them are owned by one of the devices d - 1, d, d + 1 (cyclically) and 2 by each of the other two, where block I is owned by device I // 6. Which of the three owns 4 changes from brick to brick. Blocks 0 and 767 touch brick 0.
All inputs are finite; a program needn't handle non-finite values.
Results may differ from a plain program's by a relative error of at most 0.00041.
Values may be sent and summed in bfloat16 or wider, within the bound.
No kernel may reach another device: no remote copies, remote signals or barrier semaphores. Data moves between devices by JAX's collectives and lax.ppermute only.
A program may use at most 128 MiB of HBM per device.

v0:
```python
import math

import jax
import jax.numpy as jnp
from jax import lax
from jax.sharding import PartitionSpec as P

FB = 128
KB = 8
CAP = 4
BLK_DEV = 6
SIDE = 16
BR_DEV = 1


omega = 2.0 / 3.0
four_pi = 4.0 * math.pi
slater = (3.0 / math.pi) ** (1.0 / 3.0)


def extended(cells, sides, width):
    for axis, dim in sides:
        count = lax.axis_size(axis)
        head = lax.slice_in_dim(cells, 0, width, axis=dim)
        tail = lax.slice_in_dim(cells, cells.shape[dim] - width, cells.shape[dim], axis=dim)
        cells = jnp.concatenate(
            [
                lax.ppermute(tail, axis, [(i, (i + 1) % count) for i in range(count)]),
                cells,
                lax.ppermute(head, axis, [((i + 1) % count, i) for i in range(count)]),
            ],
            axis=dim,
        )
    return cells


def from_behind(value, axis, steps):
    count = lax.axis_size(axis)
    pairs = [(source, (source + steps) % count) for source in range(count)]
    return lax.ppermute(value, axis, pairs)


def periodic(distance, period):
    return jnp.mod(distance + 0.5 * period, period) - 0.5 * period


def basis_values(device, z_slot, blocks, center_x, center_y, center_z, exponent, devices):
    functions = (blocks[:, None] * FB + jnp.arange(FB, dtype=jnp.int32)[None, :]).reshape(-1)
    owner_dev = functions // (BLK_DEV * FB)
    offset = (jnp.mod(device - owner_dev + 1, devices) - 1).astype(jnp.float32)
    grid_points = (jnp.arange(SIDE, dtype=jnp.float32) + 0.5) / SIDE
    decay_rate = exponent[functions][:, None]
    along_x = offset[:, None] + grid_points[None, :] - center_x[functions][:, None]
    along_y = periodic(grid_points[None, :] - center_y[functions][:, None], 1.0)
    along_z = periodic(z_slot + grid_points[None, :] - center_z[functions][:, None], 1.0 * BR_DEV)
    factor_x = jnp.exp(-decay_rate * along_x * along_x)
    factor_y = jnp.exp(-decay_rate * along_y * along_y)
    factor_z = jnp.exp(-decay_rate * along_z * along_z)
    values = factor_x[:, :, None, None] * factor_y[:, None, :, None] * factor_z[:, None, None, :]
    return values.reshape(functions.shape[0], SIDE * SIDE * SIDE).astype(jnp.bfloat16)


def brick_basis(device, blocks, center_x, center_y, center_z, exponent, devices):
    z_slots = jnp.arange(blocks.shape[0], dtype=jnp.float32)
    return jax.vmap(
        lambda z_slot, brick_row: basis_values(
            device, z_slot, brick_row, center_x, center_y, center_z, exponent, devices
        )
    )(z_slots, blocks)


def owned_slots(blocks, holder, devices):
    owner_dev = blocks // BLK_DEV
    held_here = (owner_dev == holder).astype(jnp.int32)
    slot_rank = jnp.cumsum(held_here, axis=1) - 1
    selected = (held_here[:, None, :] == 1) & (
        slot_rank[:, None, :] == jnp.arange(CAP, dtype=jnp.int32)[None, :, None]
    )
    is_valid = jnp.any(selected, axis=2)
    slot_pick = jnp.sum(
        selected.astype(jnp.int32) * jnp.arange(KB, dtype=jnp.int32)[None, None, :], axis=2
    )
    row_blocks = jnp.take_along_axis(blocks, slot_pick, axis=1) % BLK_DEV
    col_blocks = jnp.mod(owner_dev - holder + 2, devices) * BLK_DEV + blocks % BLK_DEV
    return (slot_pick, row_blocks, col_blocks, is_valid)


def pack_rows(density_tiles, row_blocks, col_blocks, is_valid):
    full_rows = jnp.take(density_tiles, row_blocks, axis=0)
    pieces = jax.vmap(lambda rows_one, cols_one: jnp.take(rows_one, cols_one, axis=2))(
        full_rows, col_blocks
    )
    pieces = jnp.where(is_valid[:, :, None, None, None], pieces, jnp.zeros_like(pieces))
    return pieces.reshape(row_blocks.shape[0], CAP, FB, KB * FB)


def scatter_rows(ham_tiles, received, row_blocks, col_blocks):
    bricks = received.shape[0]
    pieces = received.reshape(bricks, CAP, FB, KB, FB)

    def spread(piece, cols_one):
        return jnp.zeros((FB, 5 * BLK_DEV, FB), jnp.float32).at[:, cols_one, :].add(piece)

    widened = jax.vmap(jax.vmap(spread, (0, None)), (0, 0))(pieces, col_blocks)
    return ham_tiles.at[row_blocks].add(widened)


def hartree_exchange(density, devices):
    bricks = density.shape[0]
    charge = lax.psum(jnp.sum(density), "dev")
    average = charge / (devices * bricks * density.shape[1])
    source = density - average
    sweep_one = omega * four_pi / 6.0 * source
    brick_cells = sweep_one.reshape(bricks, SIDE, SIDE, SIDE)
    padded = extended(brick_cells, (("dev", 1),), 1)
    beside_all = padded[:, 2:] + padded[:, :-2]
    beside_all = beside_all + jnp.roll(brick_cells, 1, 2) + jnp.roll(brick_cells, -1, 2)
    z_line = brick_cells.transpose(1, 2, 0, 3).reshape(SIDE, SIDE, bricks * SIDE)
    z_sum = (
        (jnp.roll(z_line, 1, 2) + jnp.roll(z_line, -1, 2))
        .reshape(SIDE, SIDE, bricks, SIDE)
        .transpose(2, 0, 1, 3)
    )
    beside_all = (beside_all + z_sum).reshape(bricks, -1)
    sweep_two = sweep_one + omega * ((four_pi * source + beside_all) / 6.0 - sweep_one)
    return sweep_two - slater * jnp.cbrt(density)


def local(density_rows, center_x, center_y, center_z, exponent, brick_blocks):
    devices = lax.axis_size("dev")
    own_index = lax.axis_index("dev")
    left_index = jnp.mod(own_index - 1, devices)
    right_index = jnp.mod(own_index + 1, devices)
    bricks = BR_DEV
    cells = SIDE * SIDE * SIDE
    scale = 64.0 / cells
    density_tiles = density_rows.reshape(BLK_DEV, FB, 5 * BLK_DEV, FB)

    def bricks_of(device):
        return lax.dynamic_slice_in_dim(brick_blocks, device * bricks, bricks, 0)

    neighbours = (left_index, own_index, right_index)
    slots_at = [owned_slots(bricks_of(device), own_index, devices) for device in neighbours]
    ham_tiles = jnp.zeros((BLK_DEV, FB, 5 * BLK_DEV, FB), jnp.float32)
    own_blocks = bricks_of(own_index)
    orbitals = brick_basis(own_index, own_blocks, center_x, center_y, center_z, exponent, devices)
    packed = [pack_rows(density_tiles, entry[1], entry[2], entry[3]) for entry in slots_at]
    from_left = from_behind(packed[2], "dev", 1)
    from_right = from_behind(packed[0], "dev", -1)
    stacked = jnp.stack([from_left, packed[1], from_right])
    owner_dev = own_blocks // BLK_DEV
    side_of = jnp.mod(owner_dev - own_index + 1, devices)
    same_owner = owner_dev[:, :, None] == owner_dev[:, None, :]
    earlier = jnp.arange(KB)[None, :] < jnp.arange(KB)[:, None]
    slot_rank = jnp.sum((same_owner & earlier[None, :, :]).astype(jnp.int32), axis=2)
    brick_rows = stacked[side_of, jnp.arange(bricks, dtype=jnp.int32)[:, None], slot_rank]
    block_density = brick_rows.reshape(bricks, KB * FB, KB * FB)
    applied = jnp.einsum(
        "bmn,bnc->bmc", block_density, orbitals, preferred_element_type=jnp.float32
    )
    density = jnp.sum(orbitals.astype(jnp.float32) * applied, axis=1)
    potential = hartree_exchange(density, devices)
    weighted = (orbitals.astype(jnp.float32) * potential[:, None, :]).astype(jnp.bfloat16)
    ham_brick = (
        jnp.einsum("bmc,bnc->bmn", weighted, orbitals, preferred_element_type=jnp.float32) * scale
    )
    ham_split = ham_brick.reshape(bricks, KB, FB, KB * FB)
    outgoing = []
    for holder in neighbours:
        slot_pick, row_blocks, col_blocks, is_valid = owned_slots(own_blocks, holder, devices)
        picked = jnp.take_along_axis(ham_split, slot_pick[:, :, None, None], axis=1)
        outgoing.append(picked * is_valid[:, :, None, None].astype(jnp.float32))
    back_from_right = from_behind(outgoing[0], "dev", -1)
    back_from_left = from_behind(outgoing[2], "dev", 1)
    for received, entry in (
        (back_from_left, slots_at[0]),
        (outgoing[1], slots_at[1]),
        (back_from_right, slots_at[2]),
    ):
        ham_tiles = scatter_rows(ham_tiles, received, entry[1], entry[2])
    return (potential, ham_tiles.reshape(BLK_DEV * FB, 5 * BLK_DEV * FB))


def solution(mesh):
    placed = (P("dev", None), P(), P(), P(), P(), P())
    return jax.shard_map(
        local,
        mesh=mesh,
        in_specs=placed,
        out_specs=(P("dev", None), P("dev", None)),
        check_vma=False,
    )
```

profile of v0, /device:TPU:0, one launch (start us, length us, event | category | flops | bytes accessed | tf_op | source)
XLA Modules:
  0.0 394.2 jit_solution(1421391047080310032)
XLA Ops:
  0.7 10.3 %reshape.1641 = bf16[6,128,30,128]{3,2,1,0:T(8,128)(2,1)} reshape(bf16[768,3840]{1,0:T(8,128)(2,1)} %param.14) | data formatting | bytes 11796480 | tf_op jit(solution)/shard_map/reshape | solution.py:137
  11.0 7.6 %copy.51 = bf16[6,128,30,128]{3,1,2,0:T(8,128)(2,1)} copy(bf16[6,128,30,128]{3,2,1,0:T(8,128)(2,1)} %reshape.1641) | data formatting | bytes 11796480 | tf_op jit(solution)/shard_map/reshape | solution.py:137
  24.9 5.6 %gather_fusion.12 = bf16[4,128,30,128]{3,1,2,0:T(8,128)(2,1)} fusion(bf16[6,128,30,128]{3,1,2,0:T(8,128)(2,1)} %copy.51, s32[1024]{0:T(1024)S(1)} %pad_clamp_fusion.3), kind=kCustom, calls=%fused_computation.7.clone | custom fusion | bytes 7864336 | tf_op jit(solution)/shard_map/jit(_take)/gather | solution.py:89
  30.5 4.5 %bitcast_select_fusion = bf16[1,4,128,30,128]{4,2,3,1,0:T(8,128)(2,1)} fusion(bf16[4,128,30,128]{3,1,2,0:T(8,128)(2,1)} %gather_fusion.12, pred[4]{0:T(512)(128)(4,1)S(1)} %get-tuple-element.69), kind=kLoop, calls=%fused_computation.32 | loop fusion | flops 1966080 | bytes 7864324 | tf_op jit(solution)/shard_map/jit(_take)/select_n | solution.py:89
  40.6 8.2 %collective-permute-start.1 = (bf16[1,4,128,1024]{2,3,1,0:T(8,128)(2,1)}, bf16[1,4,128,1024]{2,3,1,0:T(8,128)(2,1)}, u32[]{:S(2)}, u32[]{:S(2)}) collective-permute-start(bf16[1,4,128,1024]{2,3,1,0:T(8,128)(2,1)} %bitcast.42), channel_id=1, source_target_pairs={{0,127},{1,0},{2,1},{3,2},{4,3},{5,4},{6,5},{7,6},{8,7},{9,8},{10,... | collective-permute-start | bytes 3145736 | tf_op jit(solution)/shard_map/ppermute | solution.py:40
  50.7 5.6 %gather_fusion.6 = bf16[4,128,30,128]{3,1,2,0:T(8,128)(2,1)} fusion(bf16[6,128,30,128]{3,1,2,0:T(8,128)(2,1)} %copy.51, s32[1024]{0:T(1024)S(1)} %pad_clamp_fusion.7), kind=kCustom, calls=%fused_computation.1.clone | custom fusion | bytes 7864336 | tf_op jit(solution)/shard_map/jit(_take)/gather | solution.py:89
  57.1 4.5 %bitcast_select_fusion.2 = bf16[1,4,128,30,128]{4,2,3,1,0:T(8,128)(2,1)} fusion(bf16[4,128,30,128]{3,1,2,0:T(8,128)(2,1)} %gather_fusion.6, pred[4]{0:T(512)(128)(4,1)S(1)} %and_bitcast_fusion.5), kind=kLoop, calls=%fused_computation.34 | loop fusion | flops 1966080 | bytes 7864324 | tf_op jit(solution)/shard_map/jit(_take)/select_n | solution.py:89
  71.9 6.2 %gather_fusion.1 = f32[1024]{0:T(1024)S(1)} fusion(f32[98304]{0:T(1024)S(1)} %copy-done, s32[1024]{0:T(1024)S(1)} %broadcast_clamp_fusion), kind=kCustom, calls=%fused_computation.13 | custom fusion | bytes 12288 | tf_op jit(solution)/shard_map/vmap()/gather | solution.py:53
  78.1 6.2 %gather_fusion = f32[1024]{0:T(1024)S(1)} fusion(f32[98304]{0:T(1024)S(1)} %copy-done.2, s32[1024]{0:T(1024)S(1)} %broadcast_clamp_fusion), kind=kCustom, calls=%fused_computation.12 | custom fusion | bytes 12288 | tf_op jit(solution)/shard_map/vmap()/gather | solution.py:52
  84.4 6.2 %gather_fusion.2 = f32[1024]{0:T(1024)S(1)} fusion(f32[98304]{0:T(1024)S(1)} %copy-done.3, s32[1024]{0:T(1024)S(1)} %broadcast_clamp_fusion), kind=kCustom, calls=%fused_computation.14 | custom fusion | bytes 12288 | tf_op jit(solution)/shard_map/vmap()/gather | solution.py:54
  90.5 6.2 %gather_fusion.3 = f32[1024]{0:T(1024)S(1)} fusion(f32[98304]{0:T(1024)S(1)} %copy-done.4, s32[1024]{0:T(1024)S(1)} %broadcast_clamp_fusion), kind=kCustom, calls=%fused_computation.15 | custom fusion | bytes 12288 | tf_op jit(solution)/shard_map/vmap()/gather | solution.py:55
  96.7 5.7 %gather_fusion.9 = bf16[4,128,30,128]{3,1,2,0:T(8,128)(2,1)} fusion(bf16[6,128,30,128]{3,1,2,0:T(8,128)(2,1)} %copy.51, s32[1024]{0:T(1024)S(1)} %pad_clamp_fusion.5), kind=kCustom, calls=%fused_computation.6.clone | custom fusion | bytes 7864336 | tf_op jit(solution)/shard_map/jit(_take)/gather | solution.py:89
  104.0 6.2 %multiply_convert_fusion.1 = bf16[1024,16,16,16]{0,3,2,1:T(8,128)(2,1)} fusion(f32[1024,16]{0,1:T(8,128)S(1)} %get-tuple-element.48, f32[1024,16,16]{0,2,1:T(8,128)S(1)} %broadcast_multiply_fusion), kind=kLoop, calls=%fused_computation.25 | loop fusion | flops 8388608 | bytes 9502720 | tf_op jit(solution)/shard_map/vmap()/convert_element_type | solution.py:60
  115.7 11.3 %copy.50 = bf16[1024,4096]{1,0:T(8,128)(2,1)} copy(bf16[1024,4096]{0,1:T(8,128)(2,1)} %bitcast.258) | data formatting | bytes 16777216 | tf_op jit(solution)/shard_map/convert_element_type | solution.py:161
  139.4 14.6 %fusion.1 = (f32[]{:T(128)}, f32[4096]{0:T(1024)S(1)}) fusion(bf16[1024,4096]{1,0:T(8,128)(2,1)} %copy.50, bf16[1024,1024]{1,0:T(8,128)(2,1)S(1)} %bitcast.268, bf16[1024,4096]{0,1:T(8,128)(2,1)} %bitcast.259), kind=kOutput, calls=%fused_computation.28 | convolution fusion | flops 8606707712 | bytes 18890756 | tf_op jit(solution)/shard_map/bmn,bnc->bmc/dot_general | solution.py:158
  154.0 67.3 %psum.7 = f32[]{:T(128)} all-reduce(f32[]{:T(128)} %get-tuple-element.4), channel_id=1, replica_groups=mesh['dev'=128] {'dev'}, use_global_device_ids=true, to_apply=%region_12.16 | all-reduce | flops 1 | bytes 8 | tf_op jit(solution)/shard_map/psum | solution.py:110
  223.0 7.2 %collective-permute-start.2 = (f32[1,1,16,16]{3,2,1,0:T(8,128)S(1)}, f32[1,1,16,16]{3,2,1,0:T(8,128)S(1)}, u32[]{:S(2)}, u32[]{:S(2)}) collective-permute-start(f32[1,1,16,16]{3,2,1,0:T(8,128)S(1)} %get-tuple-element.33), channel_id=1, source_target_pairs={{1,0},{2,1},{3,2},{4,3},{5,4},{6,5},{7,6},{8,7},{9,8},{10,9},{11,1... | collective-permute-start | bytes 3080 | tf_op jit(solution)/shard_map/ppermute | solution.py:30
  231.7 11.2 %bitcast_multiply_fusion = f32[1024,1024]{1,0:T(8,128)} fusion(f32[16,16,16]{2,1,0:T(8,128)S(1)} %get-tuple-element.19, f32[1024,16]{0,1:T(8,128)S(1)} %copy-done.10, f32[1024,16,16]{0,2,1:T(8,128)S(1)} %copy-done.7), kind=kOutput, calls=%fused_computation.31 | convolution fusion | flops 8620343296 | bytes 5324800 | tf_op jit(solution)/shard_map/bmc,bnc->bmn/dot_general | solution.py:165
  242.9 3.0 gather_fusion.14
  252.2 7.3 %collective-permute-start.5 = (f32[1,4,128,1024]{3,2,1,0:T(8,128)}, f32[1,4,128,1024]{3,2,1,0:T(8,128)}, u32[]{:S(2)}, u32[]{:S(2)}) collective-permute-start(f32[1,4,128,1024]{3,2,1,0:T(8,128)} %fusion.4), channel_id=1, source_target_pairs={{0,127},{1,0},{2,1},{3,2},{4,3},{5,4},{6,5},{7,6},{8,7},{9,8},{10,... | collective-permute-start | bytes 6291464 | tf_op jit(solution)/shard_map/ppermute | solution.py:40
  269.1 4.1 %broadcast.1487.clone.1 = f32[4,128,30,128]{3,1,2,0:T(8,128)} broadcast(f32[]{:T(128)} %constant.216.clone.1), dimensions={} | broadcast | bytes 7864324 | tf_op jit(solution)/shard_map/broadcast.68
  273.2 4.4 %scatter_fusion.4 = f32[4,128,30,128]{3,1,2,0:T(8,128)} fusion(f32[4,128,30,128]{3,1,2,0:T(8,128)} %broadcast.1487.clone.1, s32[8]{0:T(128)S(1)} %copy-done.31, f32[8,4,128,128]{3,2,1,0:T(8,128)S(1)} %copy.63), kind=kCustom, calls=%fused_computation.21 | custom fusion | flops 524288 | bytes 6291488 | tf_op jit(solution)/shard_map/vmap(vmap())/scatter-add | solution.py:102
  288.3 4.1 %broadcast.1487.clone = f32[4,128,30,128]{3,1,2,0:T(8,128)} broadcast(f32[]{:T(128)} %constant.216.clone.1), dimensions={} | broadcast | bytes 7864324 | tf_op jit(solution)/shard_map/broadcast.68
  292.4 5.1 %scatter_fusion.3 = f32[4,128,30,128]{3,1,2,0:T(8,128)} fusion(f32[4,128,30,128]{3,1,2,0:T(8,128)} %broadcast.1487.clone, s32[8]{0:T(128)S(1)} %copy-done.30, f32[8,4,128,128]{3,2,1,0:T(8,128)} %copy.61), kind=kCustom, calls=%fused_computation.20 | custom fusion | flops 524288 | bytes 6291488 | tf_op jit(solution)/shard_map/vmap(vmap())/scatter-add | solution.py:102
  297.5 6.0 %broadcast_in_dim.67 = f32[6,128,30,128]{3,1,2,0:T(8,128)} broadcast(f32[]{:T(128)} %constant.216.clone.1), dimensions={} | broadcast | bytes 11796484 | tf_op jit(solution)/shard_map/broadcast_in_dim | solution.py:144
  303.5 15.0 %scatter_fusion = f32[6,128,30,128]{3,1,2,0:T(8,128)} fusion(f32[6,128,30,128]{3,1,2,0:T(8,128)} %broadcast_in_dim.67, s32[4]{0:T(128)S(1)} %copy-done.22, f32[4,128,30,128]{3,1,2,0:T(8,128)} %scatter_fusion.3), kind=kCustom, calls=%fused_computation.17 | custom fusion | flops 1966080 | bytes 23592976 | tf_op jit(solution)/shard_map/scatter-add | solution.py:105
  318.5 15.0 %scatter_fusion.1 = f32[6,128,30,128]{3,1,2,0:T(8,128)} fusion(f32[6,128,30,128]{3,1,2,0:T(8,128)} %scatter_fusion, s32[4]{0:T(128)S(1)} %copy-done.19, f32[4,128,30,128]{3,1,2,0:T(8,128)} %scatter_fusion.4), kind=kCustom, calls=%fused_computation.18 | custom fusion | flops 1966080 | bytes 23592976 | tf_op jit(solution)/shard_map/scatter-add | solution.py:105
  333.5 4.1 %broadcast.1487.clone.2 = f32[4,128,30,128]{3,1,2,0:T(8,128)} broadcast(f32[]{:T(128)} %constant.216.clone.1), dimensions={} | broadcast | bytes 7864324 | tf_op jit(solution)/shard_map/broadcast.68
  337.5 4.4 %scatter_fusion.5 = f32[4,128,30,128]{3,1,2,0:T(8,128)} fusion(f32[4,128,30,128]{3,1,2,0:T(8,128)} %broadcast.1487.clone.2, s32[8]{0:T(128)S(1)} %copy-done.25, f32[8,4,128,128]{3,2,1,0:T(8,128)S(1)} %copy.65), kind=kCustom, calls=%fused_computation.22 | custom fusion | flops 524288 | bytes 6291488 | tf_op jit(solution)/shard_map/vmap(vmap())/scatter-add | solution.py:102
  341.9 15.1 %scatter_fusion.2 = f32[6,128,30,128]{3,1,2,0:T(8,128)} fusion(f32[6,128,30,128]{3,1,2,0:T(8,128)} %scatter_fusion.1, s32[4]{0:T(128)S(1)} %copy-done.24, f32[4,128,30,128]{3,1,2,0:T(8,128)} %scatter_fusion.5), kind=kCustom, calls=%fused_computation.19 | custom fusion | flops 1966080 | bytes 23592976 | tf_op jit(solution)/shard_map/scatter-add | solution.py:105
  357.1 15.7 %copy.66 = f32[6,128,30,128]{3,2,1,0:T(8,128)} copy(f32[6,128,30,128]{3,1,2,0:T(8,128)} %scatter_fusion.2) | data formatting | bytes 23592960 | tf_op jit(solution)/shard_map/scatter-add | solution.py:105
  372.8 21.0 %copy.70 = f32[96,8,30,128]{3,1,2,0:T(8,128)} copy(f32[96,8,30,128]{3,2,1,0:T(8,128)} %bitcast.257) | data formatting | bytes 23592960
  (213 shorter events, 73.0 us)
Async XLA Ops:
  0.6 71.2 %copy-start = (f32[98304]{0:T(1024)S(1)}, f32[98304]{0:T(1024)}, u32[]{:S(2)}) copy-start(f32[98304]{0:T(1024)} %param.15) | copy-start | bytes 1179652
  11.0 7.6 %copy-start.13 = (s32[128,8]{0,1:T(8,128)S(1)}, s32[128,8]{0,1:T(8,128)}, u32[]{:S(2)}) copy-start(s32[128,8]{0,1:T(8,128)} %param.19) | copy-start | bytes 12292
  21.4 17.1 %copy-start.27 = (pred[8]{0:T(512)(128)(4,1)}, pred[8]{0:T(512)(128)(4,1)S(1)}, u32[]{:S(2)}) copy-start(pred[8]{0:T(512)(128)(4,1)S(1)} %get-tuple-element.17) | copy-start | bytes 28
  24.9 13.6 %copy-start.41 = (s32[8]{0:T(128)}, s32[8]{0:T(128)S(1)}, u32[]{:S(2)}) copy-start(s32[8]{0:T(128)S(1)} %add_bitcast_fusion.2) | copy-start | bytes 100
  40.6 90.5 %collective-permute-start.1 = (bf16[1,4,128,1024]{2,3,1,0:T(8,128)(2,1)}, bf16[1,4,128,1024]{2,3,1,0:T(8,128)(2,1)}, u32[]{:S(2)}, u32[]{:S(2)}) collective-permute-start(bf16[1,4,128,1024]{2,3,1,0:T(8,128)(2,1)} %bitcast.42), channel_id=1, source_target_pairs={{0,127},{1,0},{2,1},{3,2},{4,3},{5,4},{6,5},{7,6},{8,7},{9,8},{10,... | collective-permute-start | bytes 3145736 | tf_op jit(solution)/shard_map/ppermute | solution.py:40
  50.0 46.7 %copy-start.18 = (s32[4]{0:T(128)}, s32[4]{0:T(128)S(1)}, u32[]{:S(2)}) copy-start(s32[4]{0:T(128)S(1)} %get-tuple-element.74) | copy-start | bytes 52
  64.4 13.6 %copy-start.2 = (f32[98304]{0:T(1024)S(1)}, f32[98304]{0:T(1024)}, u32[]{:S(2)}) copy-start(f32[98304]{0:T(1024)} %param.18) | copy-start | bytes 1179652
  65.9 65.2 %collective-permute-start = (bf16[1,4,128,1024]{2,3,1,0:T(8,128)(2,1)}, bf16[1,4,128,1024]{2,3,1,0:T(8,128)(2,1)S(1)}, u32[]{:S(2)}, u32[]{:S(2)}) collective-permute-start(bf16[1,4,128,1024]{2,3,1,0:T(8,128)(2,1)} %bitcast.17), channel_id=1, source_target_pairs={{0,1},{1,2},{2,3},{3,4},{4,5},{5,6},{6,7},{7,8},{8,9},{9,10},{10,1... | collective-permute-start | bytes 3145736 | tf_op jit(solution)/shard_map/ppermute | solution.py:40
  67.6 35.0 %copy-start.42 = (s32[4]{0:T(128)}, s32[4]{0:T(128)S(1)}, u32[]{:S(2)}) copy-start(s32[4]{0:T(128)S(1)} %select_reduce_fusion.1) | copy-start | bytes 52
  71.9 12.4 %copy-start.20 = (s32[8]{0:T(128)S(1)}, s32[8]{0:T(128)}, u32[]{:S(2)}) copy-start(s32[8]{0:T(128)} %get-tuple-element.8) | copy-start | bytes 100
  71.9 12.5 %copy-start.3 = (f32[98304]{0:T(1024)S(1)}, f32[98304]{0:T(1024)}, u32[]{:S(2)}) copy-start(f32[98304]{0:T(1024)} %param.16) | copy-start | bytes 1179652
  78.1 12.5 %copy-start.4 = (f32[98304]{0:T(1024)S(1)}, f32[98304]{0:T(1024)}, u32[]{:S(2)}) copy-start(f32[98304]{0:T(1024)} %param.17) | copy-start | bytes 1179652
  103.8 6.3 %copy-start.9 = (f32[1024,16]{0,1:T(8,128)}, f32[1024,16]{0,1:T(8,128)S(1)}, u32[]{:S(2)}) copy-start(f32[1024,16]{0,1:T(8,128)S(1)} %get-tuple-element.48) | copy-start | bytes 196612
  104.0 6.2 %copy-start.6 = (f32[1024,16,16]{0,2,1:T(8,128)}, f32[1024,16,16]{0,2,1:T(8,128)S(1)}, u32[]{:S(2)}) copy-start(f32[1024,16,16]{0,2,1:T(8,128)S(1)} %broadcast_multiply_fusion) | copy-start | bytes 3145732
  115.6 12.7 %copy-start.40 = (pred[4]{0:T(512)(128)(4,1)S(1)}, pred[4]{0:T(512)(128)(4,1)}, u32[]{:S(2)}) copy-start(pred[4]{0:T(512)(128)(4,1)} %get-tuple-element.77) | copy-start | bytes 16
  115.6 13.2 %copy-start.45 = (pred[4]{0:T(512)(128)(4,1)S(1)}, pred[4]{0:T(512)(128)(4,1)}, u32[]{:S(2)}) copy-start(pred[4]{0:T(512)(128)(4,1)} %fusion.61) | copy-start | bytes 16
  115.6 13.8 %copy-start.44 = (s32[4]{0:T(128)S(1)}, s32[4]{0:T(128)}, u32[]{:S(2)}) copy-start(s32[4]{0:T(128)} %select_reduce_fusion) | copy-start | bytes 52
  115.7 14.4 %copy-start.43 = (s32[4]{0:T(128)S(1)}, s32[4]{0:T(128)}, u32[]{:S(2)}) copy-start(s32[4]{0:T(128)} %copy-done.42) | copy-start | bytes 52
  154.0 77.7 %copy-start.7 = (f32[1024,16,16]{0,2,1:T(8,128)S(1)}, f32[1024,16,16]{0,2,1:T(8,128)}, u32[]{:S(2)}) copy-start(f32[1024,16,16]{0,2,1:T(8,128)} %copy-done.6) | copy-start | bytes 3145732
  154.0 77.7 %copy-start.10 = (f32[1024,16]{0,1:T(8,128)S(1)}, f32[1024,16]{0,1:T(8,128)}, u32[]{:S(2)}) copy-start(f32[1024,16]{0,1:T(8,128)} %copy-done.9) | copy-start | bytes 196612
  222.1 9.5 %copy-start.11 = (f32[4096]{0:T(1024)}, f32[4096]{0:T(1024)S(1)}, u32[]{:S(2)}) copy-start(f32[4096]{0:T(1024)S(1)} %get-tuple-element.45) | copy-start | bytes 49156
  222.1 9.5 %copy-start.14 = (f32[4096]{0:T(1024)}, f32[4096]{0:T(1024)S(1)}, u32[]{:S(2)}) copy-start(f32[4096]{0:T(1024)S(1)} %get-tuple-element.43) | copy-start | bytes 49156
  222.1 9.5 %copy-start.16 = (f32[4096]{0:T(1024)}, f32[4096]{0:T(1024)S(1)}, u32[]{:S(2)}) copy-start(f32[4096]{0:T(1024)S(1)} %get-tuple-element.44) | copy-start | bytes 49156
  222.5 9.0 %collective-permute-start.3 = (f32[1,1,16,16]{3,2,1,0:T(8,128)S(1)}, f32[1,1,16,16]{3,2,1,0:T(8,128)S(1)}, u32[]{:S(2)}, u32[]{:S(2)}) collective-permute-start(f32[1,1,16,16]{3,2,1,0:T(8,128)S(1)} %get-tuple-element.34), channel_id=1, source_target_pairs={{0,1},{1,2},{2,3},{3,4},{4,5},{5,6},{6,7},{7,8},{8,9},{9,10},{10,1... | collective-permute-start | bytes 3080 | tf_op jit(solution)/shard_map/ppermute | solution.py:28
  223.0 8.5 %collective-permute-start.2 = (f32[1,1,16,16]{3,2,1,0:T(8,128)S(1)}, f32[1,1,16,16]{3,2,1,0:T(8,128)S(1)}, u32[]{:S(2)}, u32[]{:S(2)}) collective-permute-start(f32[1,1,16,16]{3,2,1,0:T(8,128)S(1)} %get-tuple-element.33), channel_id=1, source_target_pairs={{1,0},{2,1},{3,2},{4,3},{5,4},{6,5},{7,6},{8,7},{9,8},{10,9},{11,1... | collective-permute-start | bytes 3080 | tf_op jit(solution)/shard_map/ppermute | solution.py:30
  247.6 12.0 %copy-start.36 = (pred[4]{0:T(512)(128)(4,1)S(1)}, pred[4]{0:T(512)(128)(4,1)}, u32[]{:S(2)}) copy-start(pred[4]{0:T(512)(128)(4,1)} %get-tuple-element.79) | copy-start | bytes 16
  247.6 12.0 %copy-start.32 = (s32[4]{0:T(128)S(1)}, s32[4]{0:T(128)}, u32[]{:S(2)}) copy-start(s32[4]{0:T(128)} %get-tuple-element.76) | copy-start | bytes 52
  247.6 31.2 %collective-permute-start.4 = (f32[1,4,128,1024]{3,2,1,0:T(8,128)}, f32[1,4,128,1024]{3,2,1,0:T(8,128)}, u32[]{:S(2)}, u32[]{:S(2)}) collective-permute-start(f32[1,4,128,1024]{3,2,1,0:T(8,128)} %fusion.6), channel_id=1, source_target_pairs={{0,1},{1,2},{2,3},{3,4},{4,5},{5,6},{6,7},{7,8},{8,9},{9,10},{10,1... | collective-permute-start | bytes 6291464 | tf_op jit(solution)/shard_map/ppermute | solution.py:40
  250.6 12.0 %copy-start.28 = (pred[4]{0:T(512)(128)(4,1)S(1)}, pred[4]{0:T(512)(128)(4,1)}, u32[]{:S(2)}) copy-start(pred[4]{0:T(512)(128)(4,1)} %get-tuple-element.68) | copy-start | bytes 16
  252.2 31.2 %collective-permute-start.5 = (f32[1,4,128,1024]{3,2,1,0:T(8,128)}, f32[1,4,128,1024]{3,2,1,0:T(8,128)}, u32[]{:S(2)}, u32[]{:S(2)}) collective-permute-start(f32[1,4,128,1024]{3,2,1,0:T(8,128)} %fusion.4), channel_id=1, source_target_pairs={{0,127},{1,0},{2,1},{3,2},{4,3},{5,4},{6,5},{7,6},{8,7},{9,8},{10,... | collective-permute-start | bytes 6291464 | tf_op jit(solution)/shard_map/ppermute | solution.py:40
  303.5 15.0 %copy-start.19 = (s32[4]{0:T(128)S(1)}, s32[4]{0:T(128)}, u32[]{:S(2)}) copy-start(s32[4]{0:T(128)} %copy-done.18) | copy-start | bytes 52
  372.8 21.0 %copy-start.1 = (f32[98304]{0:T(1024)S(1)}, f32[98304]{0:T(1024)}, u32[]{:S(2)}) copy-start(f32[98304]{0:T(1024)} %param.15) | copy-start | bytes 1179652
  (20 other events, 84.6 us)
where the time goes:
time: 402 us; the launch traced here: 394 us
  local copies, waits for them, and re-layouts  170 us (42%)
  other arithmetic  103 us (26%)
  blocking collectives  67.3 us (17%)
  matrix products  25.8 us (6%)
  starting transfers between devices  23.4 us (6%)
    psum x1, blocking collectives, hartree_exchange(): charge = lax.psum(jnp.sum(density), 'dev')  67.3 us
    scatter-add x3, other arithmetic, scatter_rows(): return ham_tiles.at[row_blocks].add(widened)  45.1 us
    unnamed x93, local copies, waits for them, and re-layouts  22.3 us
    reshape x2, local copies, waits for them, and re-layouts, local(): density_tiles = density_rows.reshape(BLK_DEV, FB, 5 * BLK_DEV, FB)  17.9 us
    gather x3, local copies, waits for them, and re-layouts, pack_rows(): full_rows = jnp.take(density_tiles, row_blocks, axis=0)  17 us
    ppermute x4, starting transfers between devices, from_behind(): return lax.ppermute(value, axis, pairs)  15.7 us
    scatter-add x1, local copies, waits for them, and re-layouts, scatter_rows(): return ham_tiles.at[row_blocks].add(widened)  15.7 us
    scatter-add x5, other arithmetic, spread(): jnp.zeros((FB, 5 * BLK_DEV, FB), jnp.float32).at[:, cols_one, :].add(piece)  15.1 us
  transfers between devices with their start and end apart: 6, of which 3 were waited for; matrix products, arithmetic and copies ran while one was open for 28% of the time, Pallas kernels for 0%

commit v1 on v0

v1 whole, which is shorter than its diff:
```python
import math

import jax
import jax.numpy as jnp
from jax import lax
from jax.experimental import pallas as pl
from jax.experimental.pallas import tpu as pltpu
from jax.sharding import PartitionSpec as P

FB = 128
KB = 8
BLK_DEV = 6
SIDE = 16
CELLS = SIDE * SIDE * SIDE
WIDE = KB * FB
CHUNK = 1024
N_CHUNK = CELLS // CHUNK
PAIR = 2 * FB

omega = 2.0 / 3.0
four_pi = 4.0 * math.pi
slater = (3.0 / math.pi) ** (1.0 / 3.0)

VMEM = pl.BlockSpec(memory_space=pltpu.VMEM)
SMEM = pl.BlockSpec(memory_space=pltpu.SMEM)
ANY = pl.BlockSpec(memory_space=pl.ANY)


def list_blocks(devices, side, bricks_ref, order_ref, count_ref):
    own = lax.axis_index("dev")
    brick = lax.rem(own + side + devices, devices)
    ids = [bricks_ref[brick, k] for k in range(KB)]
    held = [(i // BLK_DEV == own).astype(jnp.int32) for i in ids]
    count = sum(held)
    first, second = jnp.int32(0), count
    for i, h in zip(ids, held):
        at = jnp.where(h == 1, first, second)
        order_ref[(side + 1) * KB + at] = i
        first, second = first + h, second + 1 - h
    count_ref[side + 1] = count


def factors(devices, side, order_ref, cx_ref, cy_ref, cz_ref, ex_ref, x_ref, y_ref, z_ref):
    own = lax.axis_index("dev")
    brick = lax.rem(own + side + devices, devices)
    points = (lax.broadcasted_iota(jnp.int32, (SIDE, FB), 0).astype(jnp.float32) + 0.5) / SIDE
    for k in range(KB):
        block = order_ref[(side + 1) * KB + k]
        offset = (lax.rem(brick - block // BLK_DEV + 1 + devices, devices) - 1).astype(jnp.float32)
        row = pl.ds(block, 1)
        decay = -ex_ref[row, :]
        lanes = pl.ds(k * FB, FB)
        along_x = (offset + points) - cx_ref[row, :]
        x_ref[:, lanes] = jnp.exp(decay * along_x * along_x)
        for c_ref, out_ref in ((cy_ref, y_ref), (cz_ref, z_ref)):
            away = points - c_ref[row, :] + 0.5
            away = away - jnp.floor(away) - 0.5
            out_ref[:, lanes] = jnp.exp(decay * away * away)


def orbital_chunk(chunk, x_ref, y_ref, z_ref, xy_ref, orb_ref):
    layers = CHUNK // (SIDE * SIDE)
    for i in range(layers):
        xy_ref[pl.ds(i * SIDE, SIDE), :] = x_ref[pl.ds(chunk * layers + i, 1), :] * y_ref[...]

    def rows(r, carry):
        for u in range(4):
            ij = r * 4 + u
            values = xy_ref[pl.ds(ij, 1), :] * z_ref[...]
            orb_ref[pl.ds(pl.multiple_of(ij * SIDE, SIDE), SIDE), :] = values.astype(jnp.bfloat16)
        return carry

    lax.fori_loop(0, layers * SIDE // 4, rows, 0)


def density_kernel(
    devices, bricks_ref, cx_ref, cy_ref, cz_ref, ex_ref, rows_ref,
    left_ref, mid_ref, right_ref, charge_ref,
    order_ref, count_ref, dens_ref, x_ref, y_ref, z_ref, xy_ref, orb_ref, part_ref, sems,
):
    own = lax.axis_index("dev")
    outs = (left_ref, mid_ref, right_ref)
    for side in (-1, 0, 1):
        list_blocks(devices, side, bricks_ref, order_ref, count_ref)
        for half in range(2):

            @pl.when(half * 2 < count_ref[side + 1])
            def _():
                def fetch(at, carry):
                    a, c = at // KB, lax.rem(at, KB)
                    row_block = order_ref[(side + 1) * KB + half * 2 + a]
                    col_block = order_ref[(side + 1) * KB + c]
                    row = lax.rem(row_block, BLK_DEV)
                    col = lax.rem(col_block // BLK_DEV - own + 2 + devices, devices) * BLK_DEV + lax.rem(col_block, BLK_DEV)
                    pltpu.make_async_copy(
                        rows_ref.at[pl.ds(pl.multiple_of(row * FB, FB), FB), pl.ds(pl.multiple_of(col * FB, FB), FB)],
                        dens_ref.at[
                            side + 1,
                            half,
                            pl.ds(pl.multiple_of(a * FB, FB), FB),
                            pl.ds(pl.multiple_of(c * FB, FB), FB),
                        ],
                        sems.at[side + 1, half],
                    ).start()
                    return carry

                lax.fori_loop(0, 2 * KB, fetch, 0)

    for side in (-1, 0, 1):
        factors(devices, side, order_ref, cx_ref, cy_ref, cz_ref, ex_ref, x_ref, y_ref, z_ref)
        halves = count_ref[side + 1] // 2
        for half in range(2):

            @pl.when(half < halves)
            def _():
                pltpu.make_async_copy(
                    rows_ref.at[pl.ds(0, PAIR), pl.ds(0, WIDE)], dens_ref.at[side + 1, half], sems.at[side + 1, half]
                ).wait()

        def one_chunk(chunk, carry):
            orbital_chunk(chunk, x_ref, y_ref, z_ref, xy_ref, orb_ref)
            part_ref[...] = jnp.zeros_like(part_ref)

            def one_half(half, inner):
                applied = lax.dot_general(
                    orb_ref[...], dens_ref[side + 1, half], (((1,), (1,)), ((), ())),
                    preferred_element_type=jnp.float32,
                )
                mine = orb_ref[:, pl.ds(pl.multiple_of(half * PAIR, PAIR), PAIR)].astype(jnp.float32)
                product = applied * mine
                part_ref[...] += product[:, :FB] + product[:, FB:]
                return inner

            lax.fori_loop(0, halves, one_half, 0)
            summed = jnp.sum(part_ref[...].T, axis=0, keepdims=True)
            outs[side + 1][:, pl.ds(pl.multiple_of(chunk * CHUNK, CHUNK), CHUNK)] = summed
            return carry

        lax.fori_loop(0, N_CHUNK, one_chunk, 0)
    total = left_ref[...] + mid_ref[...] + right_ref[...]
    charge = total[:, :FB]
    for k in range(1, CELLS // FB):
        charge = charge + total[:, k * FB : (k + 1) * FB]
    charge_ref[...] = charge


def add_kernel(a_ref, b_ref, c_ref, dens_ref, head_ref, tail_ref):
    dens = a_ref[...] + b_ref[...] + c_ref[...]
    dens_ref[...] = dens
    head_ref[...] = dens[:, : SIDE * SIDE]
    tail_ref[...] = dens[:, CELLS - SIDE * SIDE :]


def potential_of(density, before, after, average):
    layer = SIDE * SIDE
    lane = lax.broadcasted_iota(jnp.int32, density.shape, 1)
    along_z = lane & (SIDE - 1)
    along_y = (lane // SIDE) & (SIDE - 1)
    scale = omega * four_pi / 6.0
    source = density - average
    one = scale * source
    padded = jnp.concatenate([scale * (before - average), one, scale * (after - average)], axis=1)
    beside = padded[:, : CELLS] + padded[:, 2 * layer :]

    def moved(steps):
        return pltpu.roll(one, steps % CELLS, 1)

    beside += jnp.where(along_y > 0, moved(SIDE), moved(SIDE - layer))
    beside += jnp.where(along_y < SIDE - 1, moved(-SIDE), moved(layer - SIDE))
    beside += jnp.where(along_z > 0, moved(1), moved(1 - SIDE))
    beside += jnp.where(along_z < SIDE - 1, moved(-1), moved(SIDE - 1))
    two = one + omega * ((four_pi * source + beside) / 6.0 - one)
    root = jnp.exp(jnp.log(jnp.abs(density)) * (1.0 / 3.0))
    return two - slater * jnp.where(density < 0.0, -root, root)


def ham_kernel(
    devices, bricks_ref, cx_ref, cy_ref, cz_ref, ex_ref,
    left_ref, mid_ref, right_ref, before_ref, after_ref, charge_ref,
    pot_ref, ham_ref,
    order_ref, count_ref, v_ref, x_ref, y_ref, z_ref, xy_ref, orb_ref, acc_ref,
):
    own = lax.axis_index("dev")
    layer = SIDE * SIDE

    def wide(ref):
        return jnp.broadcast_to(ref[...], (8, ref.shape[1]))

    average = jnp.sum(charge_ref[...]) / (devices * CELLS)
    left, mid, right = wide(left_ref), wide(mid_ref), wide(right_ref)
    v_ref[0] = potential_of(left, wide(before_ref), mid[:, :layer], average)
    own_potential = potential_of(mid, left[:, CELLS - layer :], right[:, :layer], average)
    v_ref[1] = own_potential
    v_ref[2] = potential_of(right, mid[:, CELLS - layer :], wide(after_ref), average)
    pot_ref[...] = own_potential[:1]
    ham_ref[...] = jnp.zeros_like(ham_ref)
    for side in (-1, 0, 1):
        list_blocks(devices, side, bricks_ref, order_ref, count_ref)
        factors(devices, side, order_ref, cx_ref, cy_ref, cz_ref, ex_ref, x_ref, y_ref, z_ref)
        halves = count_ref[side + 1] // 2
        acc_ref[...] = jnp.zeros_like(acc_ref)

        def one_chunk(chunk, carry):
            orbital_chunk(chunk, x_ref, y_ref, z_ref, xy_ref, orb_ref)
            v = v_ref[side + 1, pl.ds(0, 1), pl.ds(pl.multiple_of(chunk * CHUNK, CHUNK), CHUNK)]

            def one_half(half, inner):
                mine = orb_ref[:, pl.ds(pl.multiple_of(half * PAIR, PAIR), PAIR)].T
                weighted = (mine.astype(jnp.float32) * v).astype(jnp.bfloat16)
                acc_ref[half] += jnp.dot(weighted, orb_ref[...], preferred_element_type=jnp.float32)
                return inner

            lax.fori_loop(0, halves, one_half, 0)
            return carry

        lax.fori_loop(0, N_CHUNK, one_chunk, 0)

        def put(at, carry):
            half, rest = at // (2 * KB), lax.rem(at, 2 * KB)
            a, c = rest // KB, lax.rem(rest, KB)
            row_block = order_ref[(side + 1) * KB + half * 2 + a]
            col_block = order_ref[(side + 1) * KB + c]
            row = lax.rem(row_block, BLK_DEV)
            col = lax.rem(col_block // BLK_DEV - own + 2 + devices, devices) * BLK_DEV + lax.rem(col_block, BLK_DEV)
            piece = acc_ref[half, pl.ds(pl.multiple_of(a * FB, FB), FB), pl.ds(pl.multiple_of(c * FB, FB), FB)]
            ham_ref[
                pl.ds(pl.multiple_of(row * FB, FB), FB), pl.ds(pl.multiple_of(col * FB, FB), FB)
            ] += piece * (64.0 / CELLS)
            return carry

        lax.fori_loop(0, halves * 2 * KB, put, 0)


def f32(*shape):
    return jax.ShapeDtypeStruct(shape, jnp.float32)


def moved_by(value, steps, devices):
    return lax.ppermute(value, "dev", [(i, (i + steps) % devices) for i in range(devices)])


def solution(mesh):
    devices = mesh.shape["dev"]

    def shared_scratch():
        return [
            pltpu.VMEM((SIDE, WIDE), jnp.float32),
            pltpu.VMEM((SIDE, WIDE), jnp.float32),
            pltpu.VMEM((SIDE, WIDE), jnp.float32),
            pltpu.VMEM((CHUNK // SIDE, WIDE), jnp.float32),
            pltpu.VMEM((CHUNK, WIDE), jnp.bfloat16),
        ]

    def lists():
        return [pltpu.SMEM((3 * KB,), jnp.int32), pltpu.SMEM((3,), jnp.int32)]

    def local(density_rows, center_x, center_y, center_z, exponent, brick_blocks):
        tables = [t.reshape(-1, FB) for t in (center_x, center_y, center_z, exponent)]
        to_left, kept, to_right, charge = pl.pallas_call(
            lambda *refs: density_kernel(devices, *refs),
            out_shape=[f32(1, CELLS), f32(1, CELLS), f32(1, CELLS), f32(1, FB)],
            in_specs=[SMEM] + [VMEM] * 4 + [ANY],
            out_specs=[VMEM] * 4,
            scratch_shapes=lists()
            + [pltpu.VMEM((3, 2, PAIR, WIDE), jnp.bfloat16)]
            + shared_scratch()
            + [pltpu.VMEM((CHUNK, FB), jnp.float32), pltpu.SemaphoreType.DMA((3, 2))],
            compiler_params=pltpu.CompilerParams(vmem_limit_bytes=48 * 2**20),
        )(brick_blocks, *tables, density_rows)
        from_right = moved_by(to_left, -1, devices)
        from_left = moved_by(to_right, 1, devices)
        steps = 1
        while steps < devices:
            charge = charge + lax.ppermute(charge, "dev", [(i, i ^ steps) for i in range(devices)])
            steps *= 2
        density, head, tail = pl.pallas_call(
            add_kernel,
            out_shape=[f32(1, CELLS), f32(1, SIDE * SIDE), f32(1, SIDE * SIDE)],
            in_specs=[VMEM] * 3,
            out_specs=[VMEM] * 3,
        )(kept, from_left, from_right)
        left = moved_by(density, 1, devices)
        right = moved_by(density, -1, devices)
        before = moved_by(tail, 2, devices)
        after = moved_by(head, -2, devices)
        return pl.pallas_call(
            lambda *refs: ham_kernel(devices, *refs),
            out_shape=[f32(1, CELLS), f32(BLK_DEV * FB, 5 * BLK_DEV * FB)],
            in_specs=[SMEM] + [VMEM] * 10,
            out_specs=[VMEM] * 2,
            scratch_shapes=lists()
            + [pltpu.VMEM((3, 8, CELLS), jnp.float32)]
            + shared_scratch()
            + [pltpu.VMEM((2, PAIR, WIDE), jnp.float32)],
            compiler_params=pltpu.CompilerParams(vmem_limit_bytes=48 * 2**20),
        )(brick_blocks, *tables, left, density, right, before, after, charge)

    def program(density_rows, center_x, center_y, center_z, exponent, brick_blocks):
        potential, ham = local(density_rows, center_x, center_y, center_z, exponent, brick_blocks)
        return potential, ham

    return jax.shard_map(
        program,
        mesh=mesh,
        in_specs=(P("dev", None), P(), P(), P(), P(), P()),
        out_specs=(P("dev", None), P("dev", None)),
        check_vma=False,
    )
```

time: 402 us -> 120 us (0.30); the launches traced: 394 us -> 120 us
  local copies, waits for them, and re-layouts: 170 us -> 10.7 us
  other arithmetic: 103 us -> 0.02 us
  blocking collectives: 67.3 us -> 0 us
  Pallas kernels: 0 us -> 61.9 us
  matrix products: 25.8 us -> 0 us
  waiting for transfers between devices: 2.53 us -> 24.3 us
    psum x1 -> x0, blocking collectives: 67.3 us -> none  [hartree_exchange(): charge = lax.psum(jnp.sum(density), 'dev')]
    gather x21 -> x0, local copies, waits for them, and re-layouts: 66 us -> none  [the longest x3 17 us: pack_rows(): full_rows = jnp.take(density_tiles, row_blocks, axis=0)]
    pallas_call x0 -> x3, Pallas kernels: none -> 61.9 us  [the longest x1 32.6 us: local(): pl.pallas_call(lambda *refs: ham_kernel(devices, *refs), out_shape=[f32(1...]
    scatter-add x8 -> x0, other arithmetic: 60.2 us -> none  [the longest x3 45.1 us: scatter_rows(): return ham_tiles.at[row_blocks].add(widened)]
    dot_general x2 -> x0, matrix products: 25.8 us -> none  [the longest x1 14.6 us: local(): jnp.einsum('bmn,bnc->bmc', block_density, orbitals, preferred_element_typ...]
    reshape x6 -> x0, local copies, waits for them, and re-layouts: 23.7 us -> none  [the longest x2 17.9 us: local(): density_tiles = density_rows.reshape(BLK_DEV, FB, 5 * BLK_DEV, FB)]
    ppermute x6 -> x13, waiting for transfers between devices: 2.53 us -> 24.3 us  [the longest x7 22.9 us: local(): lax.ppermute(charge, 'dev', [(i, i ^ steps) for i in range(devices)])]
    scatter-add x1 -> x0, local copies, waits for them, and re-layouts: 15.7 us -> none  [scatter_rows(): return ham_tiles.at[row_blocks].add(widened)]
  transfers between devices with their start and end apart: 6 -> 13, of which waited for: 3 -> 7; matrix products, arithmetic and copies ran while one was open for 28% -> 0% of each run, Pallas kernels for 0% -> 0%
where the time goes in v1:
time: 120 us
  Pallas kernels  61.9 us (52%)
  waiting for transfers between devices  24.3 us (20%)
  starting transfers between devices  22.3 us (19%)
  local copies, waits for them, and re-layouts  10.7 us (9%)
    pallas_call x1, Pallas kernels, local(): pl.pallas_call(lambda *refs: ham_kernel(devices, *refs), out_shape=[f32(1...  32.6 us
    pallas_call x1, Pallas kernels, local(): pl.pallas_call(lambda *refs: density_kernel(devices, *refs), out_shape=[f...  27.9 us
    ppermute x7, waiting for transfers between devices, local(): lax.ppermute(charge, 'dev', [(i, i ^ steps) for i in range(devices)])  22.9 us
    ppermute x6, starting transfers between devices, moved_by(): lax.ppermute(value, 'dev', [(i, (i + steps) % devices) for i in range(dev...  21.8 us
    unnamed x25, local copies, waits for them, and re-layouts  10.7 us
  transfers between devices with their start and end apart: 13, of which 7 were waited for; matrix products, arithmetic and copies ran while one was open for 0% of the time, Pallas kernels for 0%

profile of v1, /device:TPU:0, one launch (start us, length us, event | category | flops | bytes accessed | tf_op | source)
XLA Modules:
  0.0 119.9 jit_solution(13761913778189550357)
XLA Ops:
  0.6 0.8 copy.9.refs_0_
  1.4 1.0 copy-done
  2.4 1.0 copy-done.2
  3.4 1.0 copy-done.4
  4.4 1.0 copy-done.6
  5.4 27.9 %shard_map.77 = (f32[1,4096]{1,0:T(1,128)S(1)}, f32[1,4096]{1,0:T(1,128)S(1)}, f32[1,4096]{1,0:T(1,128)S(1)}, f32[1,128]{1,0:T(1,128)S(1)}) custom-call(s32[128,8]{1,0:T(8,128)S(1)} %copy.9.refs_0_, f32[768,128]{1,0:T(8,128)S(1)} %bitcast.4, f32[768,128]{1,0:T(8,128)S(1)} %bitcast.6, f32[768,128]{1,0:T(8,128)S(1)} %bitcast.8, f32[768,128]{1,0:T(8,128)S(1)} %bitcast.10, ...), custom_call_target="tpu_custom_call" | custom-call | tf_op jit(solution)/shard_map/pallas_call | solution.py:259
  33.4 0.0 copy-start.9
  33.4 0.6 copy-done.9
  34.0 7.2 %collective-permute-start.1 = (f32[1,4096]{1,0:T(1,128)S(1)}, f32[1,4096]{1,0:T(1,128)S(1)}, u32[]{:S(2)}, u32[]{:S(2)}) collective-permute-start(f32[1,4096]{1,0:T(1,128)S(1)} %get-tuple-element.11), channel_id=1, source_target_pairs={{0,127},{1,0},{2,1},{3,2},{4,3},{5,4},{6,5},{7,6},{8,7},{9,8},{10,... | collective-permute-start | bytes 49160 | tf_op jit(solution)/shard_map/ppermute | solution.py:239
  41.1 1.4 %collective-permute-done.b_ref = f32[1,4096]{1,0:T(1,128)S(1)} collective-permute-done((f32[1,4096]{1,0:T(1,128)S(1)}, f32[1,4096]{1,0:T(1,128)S(1)}, u32[]{:S(2)}, u32[]{:S(2)}) %collective-permute-start) | collective-permute-done | bytes 16416 | tf_op jit(solution)/shard_map/ppermute | solution.py:239
  42.6 0.0 collective-permute-done.1.c_ref
  42.6 0.6 copy-done.10
  43.2 0.0 copy-done.11
  43.2 1.4 %shard_map.78 = (f32[1,4096]{1,0:T(1,128)}, f32[1,256]{1,0:T(1,128)}, f32[1,256]{1,0:T(1,128)}) custom-call(f32[1,4096]{1,0:T(1,128)} %copy-done.9, f32[1,4096]{1,0:T(1,128)} %copy-done.10, f32[1,4096]{1,0:T(1,128)} %copy-done.11), custom_call_target="tpu_custom_call" | custom-call | tf_op jit(solution)/shard_map/pallas_call | solution.py:276
  44.5 7.2 %collective-permute-start.3 = (f32[1,4096]{1,0:T(1,128)}, f32[1,4096]{1,0:T(1,128)S(1)}, u32[]{:S(2)}, u32[]{:S(2)}) collective-permute-start(f32[1,4096]{1,0:T(1,128)} %get-tuple-element.12.refs_6_), channel_id=1, source_target_pairs={{0,127},{1,0},{2,1},{3,2},{4,3},{5,4},{6,5},{7,6},{8,7},{9,8},{10,... | collective-permute-start | bytes 49160 | tf_op jit(solution)/shard_map/ppermute | solution.py:239
  51.7 0.0 collective-permute-start.2
  51.7 1.1 collective-permute-done.6
  52.8 3.5 %collective-permute-done.7 = f32[1,128]{1,0:T(1,128)S(1)} collective-permute-done((f32[1,128]{1,0:T(1,128)S(1)}, f32[1,128]{1,0:T(1,128)S(1)}, u32[]{:S(2)}, u32[]{:S(2)}) %collective-permute-start.7) | collective-permute-done | bytes 544 | tf_op jit(solution)/shard_map/ppermute | solution.py:274
  56.4 5.0 %collective-permute-done.8 = f32[1,128]{1,0:T(1,128)S(1)} collective-permute-done((f32[1,128]{1,0:T(1,128)S(1)}, f32[1,128]{1,0:T(1,128)S(1)}, u32[]{:S(2)}, u32[]{:S(2)}) %collective-permute-start.8) | collective-permute-done | bytes 544 | tf_op jit(solution)/shard_map/ppermute | solution.py:274
  61.4 3.5 %collective-permute-done.9 = f32[1,128]{1,0:T(1,128)S(1)} collective-permute-done((f32[1,128]{1,0:T(1,128)S(1)}, f32[1,128]{1,0:T(1,128)S(1)}, u32[]{:S(2)}, u32[]{:S(2)}) %collective-permute-start.9) | collective-permute-done | bytes 544 | tf_op jit(solution)/shard_map/ppermute | solution.py:274
  65.0 5.0 %collective-permute-done.10 = f32[1,128]{1,0:T(1,128)S(1)} collective-permute-done((f32[1,128]{1,0:T(1,128)S(1)}, f32[1,128]{1,0:T(1,128)S(1)}, u32[]{:S(2)}, u32[]{:S(2)}) %collective-permute-start.10) | collective-permute-done | bytes 544 | tf_op jit(solution)/shard_map/ppermute | solution.py:274
  70.0 0.0 collective-permute-start.4
  70.0 7.4 %collective-permute-start.5 = (f32[1,256]{1,0:T(1,128)}, f32[1,256]{1,0:T(1,128)S(1)}, u32[]{:S(2)}, u32[]{:S(2)}) collective-permute-start(f32[1,256]{1,0:T(1,128)} %get-tuple-element.14), channel_id=1, source_target_pairs={{0,126},{1,127},{2,0},{3,1},{4,2},{5,3},{6,4},{7,5},{8,6},{9,7},{1... | collective-permute-start | bytes 3080 | tf_op jit(solution)/shard_map/ppermute | solution.py:239
  77.5 0.5 collective-permute-start.12
  77.9 4.6 %collective-permute-done.12 = f32[1,128]{1,0:T(1,128)S(1)} collective-permute-done((f32[1,128]{1,0:T(1,128)S(1)}, f32[1,128]{1,0:T(1,128)S(1)}, u32[]{:S(2)}, u32[]{:S(2)}) %collective-permute-start.12) | collective-permute-done | bytes 544 | tf_op jit(solution)/shard_map/ppermute | solution.py:274
  82.6 0.0 copy-start.1
  82.6 1.0 copy-done.1
  83.6 1.0 copy-done.3
  84.6 1.0 copy-done.5
  85.5 1.0 copy-done.7
  86.5 0.7 copy-done.8
  87.3 32.6 %shard_map.79 = (f32[1,4096]{1,0:T(1,128)}, f32[768,3840]{1,0:T(8,128)}) custom-call(s32[128,8]{1,0:T(8,128)S(1)} %copy.9.refs_0_, f32[768,128]{1,0:T(8,128)S(1)} %bitcast.5, f32[768,128]{1,0:T(8,128)S(1)} %bitcast.7, f32[768,128]{1,0:T(8,128)S(1)} %bitcast.9, f32[768,128]{1,0:T(8,128)S(1)} %bitcast.11, f32[1,4096]{1,0:T(1,128)S(1)} %collective-permute-done.2.refs_5_, ...), custom_call_target="tpu_custom_call" | custom-call | tf_op jit(solution)/shard_map/pallas_call | solution.py:286
  (29 shorter events, 0.1 us)
Async XLA Ops:
  1.4 1.0 copy-start
  2.4 1.0 copy-start.2
  3.4 1.0 copy-start.4
  4.4 1.0 copy-start.6
  33.4 0.6 copy-start.9
  34.0 8.6 %collective-permute-start = (f32[1,4096]{1,0:T(1,128)S(1)}, f32[1,4096]{1,0:T(1,128)S(1)}, u32[]{:S(2)}, u32[]{:S(2)}) collective-permute-start(f32[1,4096]{1,0:T(1,128)S(1)} %get-tuple-element.10), channel_id=1, source_target_pairs={{0,1},{1,2},{2,3},{3,4},{4,5},{5,6},{6,7},{7,8},{8,9},{9,10},{10,1... | collective-permute-start | bytes 49160 | tf_op jit(solution)/shard_map/ppermute | solution.py:239
  34.0 8.6 %collective-permute-start.1 = (f32[1,4096]{1,0:T(1,128)S(1)}, f32[1,4096]{1,0:T(1,128)S(1)}, u32[]{:S(2)}, u32[]{:S(2)}) collective-permute-start(f32[1,4096]{1,0:T(1,128)S(1)} %get-tuple-element.11), channel_id=1, source_target_pairs={{0,127},{1,0},{2,1},{3,2},{4,3},{5,4},{6,5},{7,6},{8,7},{9,8},{10,... | collective-permute-start | bytes 49160 | tf_op jit(solution)/shard_map/ppermute | solution.py:239
  42.6 0.6 copy-start.10
  42.6 0.6 copy-start.11
  44.5 38.0 %collective-permute-start.3 = (f32[1,4096]{1,0:T(1,128)}, f32[1,4096]{1,0:T(1,128)S(1)}, u32[]{:S(2)}, u32[]{:S(2)}) collective-permute-start(f32[1,4096]{1,0:T(1,128)} %get-tuple-element.12.refs_6_), channel_id=1, source_target_pairs={{0,127},{1,0},{2,1},{3,2},{4,3},{5,4},{6,5},{7,6},{8,7},{9,8},{10,... | collective-permute-start | bytes 49160 | tf_op jit(solution)/shard_map/ppermute | solution.py:239
  51.7 30.9 %collective-permute-start.2 = (f32[1,4096]{1,0:T(1,128)}, f32[1,4096]{1,0:T(1,128)S(1)}, u32[]{:S(2)}, u32[]{:S(2)}) collective-permute-start(f32[1,4096]{1,0:T(1,128)} %get-tuple-element.12.refs_6_), channel_id=1, source_target_pairs={{0,1},{1,2},{2,3},{3,4},{4,5},{5,6},{6,7},{7,8},{8,9},{9,10},{10,1... | collective-permute-start | bytes 49160 | tf_op jit(solution)/shard_map/ppermute | solution.py:239
  51.7 1.1 collective-permute-start.6
  52.8 3.5 %collective-permute-start.7 = (f32[1,128]{1,0:T(1,128)S(1)}, f32[1,128]{1,0:T(1,128)S(1)}, u32[]{:S(2)}, u32[]{:S(2)}) collective-permute-start(f32[1,128]{1,0:T(1,128)S(1)} %add.21), channel_id=1, source_target_pairs={{0,2},{1,3},{2,0},{3,1},{4,6},{5,7},{6,4},{7,5},{8,10},{9,11},{10,... | collective-permute-start | bytes 1544 | tf_op jit(solution)/shard_map/ppermute | solution.py:274
  56.4 5.0 %collective-permute-start.8 = (f32[1,128]{1,0:T(1,128)S(1)}, f32[1,128]{1,0:T(1,128)S(1)}, u32[]{:S(2)}, u32[]{:S(2)}) collective-permute-start(f32[1,128]{1,0:T(1,128)S(1)} %add.22), channel_id=1, source_target_pairs={{0,4},{1,5},{2,6},{3,7},{4,0},{5,1},{6,2},{7,3},{8,12},{9,13},{10,... | collective-permute-start | bytes 1544 | tf_op jit(solution)/shard_map/ppermute | solution.py:274
  61.4 3.5 %collective-permute-start.9 = (f32[1,128]{1,0:T(1,128)S(1)}, f32[1,128]{1,0:T(1,128)S(1)}, u32[]{:S(2)}, u32[]{:S(2)}) collective-permute-start(f32[1,128]{1,0:T(1,128)S(1)} %add.23), channel_id=1, source_target_pairs={{0,8},{1,9},{2,10},{3,11},{4,12},{5,13},{6,14},{7,15},{8,0},{9,1},... | collective-permute-start | bytes 1544 | tf_op jit(solution)/shard_map/ppermute | solution.py:274
  65.0 5.0 %collective-permute-start.10 = (f32[1,128]{1,0:T(1,128)S(1)}, f32[1,128]{1,0:T(1,128)S(1)}, u32[]{:S(2)}, u32[]{:S(2)}) collective-permute-start(f32[1,128]{1,0:T(1,128)S(1)} %add.24), channel_id=1, source_target_pairs={{0,16},{1,17},{2,18},{3,19},{4,20},{5,21},{6,22},{7,23},{8,24},{9,... | collective-permute-start | bytes 1544 | tf_op jit(solution)/shard_map/ppermute | solution.py:274
  70.0 7.5 %collective-permute-start.11 = (f32[1,128]{1,0:T(1,128)S(1)}, f32[1,128]{1,0:T(1,128)S(1)}, u32[]{:S(2)}, u32[]{:S(2)}) collective-permute-start(f32[1,128]{1,0:T(1,128)S(1)} %add.25), channel_id=1, source_target_pairs={{0,32},{1,33},{2,34},{3,35},{4,36},{5,37},{6,38},{7,39},{8,40},{9,... | collective-permute-start | bytes 1544 | tf_op jit(solution)/shard_map/ppermute | solution.py:274
  70.0 12.5 %collective-permute-start.4 = (f32[1,256]{1,0:T(1,128)}, f32[1,256]{1,0:T(1,128)S(1)}, u32[]{:S(2)}, u32[]{:S(2)}) collective-permute-start(f32[1,256]{1,0:T(1,128)} %get-tuple-element.13), channel_id=1, source_target_pairs={{0,2},{1,3},{2,4},{3,5},{4,6},{5,7},{6,8},{7,9},{8,10},{9,11},{10,... | collective-permute-start | bytes 3080 | tf_op jit(solution)/shard_map/ppermute | solution.py:239
  70.0 12.5 %collective-permute-start.5 = (f32[1,256]{1,0:T(1,128)}, f32[1,256]{1,0:T(1,128)S(1)}, u32[]{:S(2)}, u32[]{:S(2)}) collective-permute-start(f32[1,256]{1,0:T(1,128)} %get-tuple-element.14), channel_id=1, source_target_pairs={{0,126},{1,127},{2,0},{3,1},{4,2},{5,3},{6,4},{7,5},{8,6},{9,7},{1... | collective-permute-start | bytes 3080 | tf_op jit(solution)/shard_map/ppermute | solution.py:239
  77.5 5.0 %collective-permute-start.12 = (f32[1,128]{1,0:T(1,128)S(1)}, f32[1,128]{1,0:T(1,128)S(1)}, u32[]{:S(2)}, u32[]{:S(2)}) collective-permute-start(f32[1,128]{1,0:T(1,128)S(1)} %add.26), channel_id=1, source_target_pairs={{0,64},{1,65},{2,66},{3,67},{4,68},{5,69},{6,70},{7,71},{8,72},{9,... | collective-permute-start | bytes 1544 | tf_op jit(solution)/shard_map/ppermute | solution.py:274
  82.6 1.0 copy-start.1
  83.6 1.0 copy-start.3
  84.5 1.0 copy-start.5
  85.5 1.0 copy-start.7
  86.5 0.7 copy-start.8

commit v2 on v1

v2 whole, which is shorter than its diff:
```python
import math

import jax
import jax.numpy as jnp
from jax import lax
from jax.experimental import pallas as pl
from jax.experimental.pallas import tpu as pltpu
from jax.sharding import PartitionSpec as P

FB = 128
KB = 8
BLK_DEV = 6
SIDE = 16
LAYER = SIDE * SIDE
CELLS = SIDE * LAYER
WIDE = KB * FB
CHUNK = 1024
SUB = 256
PAIR = 2 * FB
TILE = 8
TILES = 5
COLS = 5 * BLK_DEV

omega = 2.0 / 3.0
four_pi = 4.0 * math.pi
slater = (3.0 / math.pi) ** (1.0 / 3.0)

VMEM = pl.BlockSpec(memory_space=pltpu.VMEM)
SMEM = pl.BlockSpec(memory_space=pltpu.SMEM)
HBM = pl.BlockSpec(memory_space=pltpu.HBM)
LIMIT = 48 * 2**20


def aligned(index, unit):
    return pl.ds(pl.multiple_of(index * unit, unit), unit)


def wrap(value, count):
    return lax.rem(value + 2 * count, count)


def list_blocks(devices, bricks_ref, order_ref, count_ref):
    own = lax.axis_index("dev")
    for side in range(3):
        brick = wrap(own + side - 1, devices)
        ids = [bricks_ref[k, brick] for k in range(KB)]
        held = [(i // BLK_DEV == own).astype(jnp.int32) for i in ids]
        first, second = jnp.int32(0), sum(held)
        count_ref[side] = second
        for i, h in zip(ids, held):
            order_ref[side * KB + jnp.where(h == 1, first, second)] = i
            first, second = first + h, second + 1 - h


def place(devices, order_ref, side, a, c):
    own = lax.axis_index("dev")
    row_block, col_block = order_ref[side * KB + a], order_ref[side * KB + c]
    col = wrap(col_block // BLK_DEV - own + 2, devices) * BLK_DEV + lax.rem(col_block, BLK_DEV)
    return lax.rem(row_block, BLK_DEV), col


def first_tile(devices):
    own = lax.axis_index("dev")
    return wrap((own - 2) * BLK_DEV, devices * BLK_DEV) // TILE


def fetch_tables(devices, table_refs, tables_ref, sem):
    base = first_tile(devices)
    for t, table_ref in enumerate(table_refs):
        for k in range(TILES):
            tile = lax.rem(base + k, devices * BLK_DEV // TILE)
            pltpu.make_async_copy(
                table_ref.at[aligned(tile, TILE), :], tables_ref.at[t, pl.ds(k * TILE, TILE), :], sem
            ).start()


def factors(devices, side, order_ref, tables_ref, x_ref, y_ref, z_ref):
    own = lax.axis_index("dev")
    brick = wrap(own + side - 1, devices)
    base = first_tile(devices) * TILE
    points = (lax.broadcasted_iota(jnp.int32, (SIDE, FB), 0).astype(jnp.float32) + 0.5) / SIDE
    for k in range(KB):
        block = order_ref[side * KB + k]
        offset = (wrap(brick - block // BLK_DEV + 1, devices) - 1).astype(jnp.float32)
        row = pl.ds(wrap(block - base, devices * BLK_DEV), 1)
        decay = -tables_ref[3, row, :]
        lanes = pl.ds(k * FB, FB)
        along_x = (offset + points) - tables_ref[0, row, :]
        x_ref[:, lanes] = jnp.exp(decay * along_x * along_x)
        for t, out_ref in ((1, y_ref), (2, z_ref)):
            away = points - tables_ref[t, row, :] + 0.5
            away = away - jnp.floor(away) - 0.5
            out_ref[:, lanes] = jnp.exp(decay * away * away)


def orbital_chunk(part, step, x_ref, y_ref, z_ref, orb_ref):
    layers = CHUNK // LAYER
    for k in range(KB):
        lanes = slice(k * FB, (k + 1) * FB)
        x = x_ref[aligned(step, 8), lanes]
        y, z = y_ref[:, lanes], z_ref[:, lanes]
        for i in range(layers):
            xy = x[part * layers + i : part * layers + i + 1] * y
            for j in range(SIDE):
                at = (i * SIDE + j) * SIDE
                orb_ref[at : at + SIDE, lanes] = (xy[j : j + 1] * z).astype(jnp.bfloat16)


def density_kernel(
    devices, bricks_ref, cx_ref, cy_ref, cz_ref, ex_ref, rows_ref,
    left_ref, mid_ref, right_ref, zero_out_ref,
    order_ref, count_ref, tables_ref, x_ref, y_ref, z_ref, orb_a, orb_b, dens_ref, zero_ref, res_ref,
    table_sem, dens_sems, zero_sems,
):
    fetch_tables(devices, (cx_ref, cy_ref, cz_ref, ex_ref), tables_ref, table_sem)
    list_blocks(devices, bricks_ref, order_ref, count_ref)

    def fetch_brick(side, carry):
        def fetch(at, inner):
            a, c = at // KB, lax.rem(at, KB)
            row, col = place(devices, order_ref, side, a, c)
            pltpu.make_async_copy(
                rows_ref.at[aligned(row, FB), aligned(col, FB)],
                dens_ref.at[side, aligned(a, FB), aligned(c, FB)],
                dens_sems.at[side, a // 2],
            ).start()
            return inner

        return lax.fori_loop(0, count_ref[side] * KB, fetch, carry)

    lax.fori_loop(0, 3, fetch_brick, 0)
    zero_ref[...] = jnp.zeros_like(zero_ref)
    zero_copies = [
        pltpu.make_async_copy(zero_ref, zero_out_ref.at[pl.ds(r * FB, FB), :], zero_sems.at[r]) for r in range(BLK_DEV)
    ]
    for copy in zero_copies:
        copy.start()
    pltpu.make_async_copy(tables_ref, tables_ref, table_sem).wait()

    def one_brick(side, carry):
        factors(devices, side, order_ref, tables_ref, x_ref, y_ref, z_ref)

        def await_half(half, inner):
            pltpu.make_async_copy(
                rows_ref.at[pl.ds(0, PAIR), pl.ds(0, WIDE)],
                dens_ref.at[side, aligned(half, PAIR), :],
                dens_sems.at[side, half],
            ).wait()
            return inner

        lax.fori_loop(0, count_ref[side] // 2, await_half, 0)

        def steps(rows):
            def step(t, inner):
                for part, orb_ref in ((0, orb_a), (1, orb_b)):
                    orbital_chunk(part, t, x_ref, y_ref, z_ref, orb_ref)
                    for s in range(0, CHUNK, SUB):
                        applied = lax.dot_general(
                            orb_ref[s : s + SUB, :], dens_ref[side, :rows, :], (((1,), (1,)), ((), ())),
                            preferred_element_type=jnp.float32,
                        )
                        product = applied * orb_ref[s : s + SUB, :rows].astype(jnp.float32)
                        total = product[:, :FB]
                        for k in range(FB, rows, FB):
                            total = total + product[:, k : k + FB]
                        at = pl.ds(pl.multiple_of(t * 2 * CHUNK + part * CHUNK + s, SUB), SUB)
                        res_ref[side, :, at] = jnp.sum(total.T, axis=0, keepdims=True)
                return inner

            lax.fori_loop(0, CELLS // (2 * CHUNK), step, 0)

        pl.when(count_ref[side] == 2)(lambda: steps(PAIR))
        pl.when(count_ref[side] != 2)(lambda: steps(2 * PAIR))
        return carry

    lax.fori_loop(0, 3, one_brick, 0)
    total = res_ref[0] + res_ref[1] + res_ref[2]
    charge = total[:, :FB]
    for k in range(1, CELLS // FB):
        charge = charge + total[:, k * FB : (k + 1) * FB]
    for side, ref in enumerate((left_ref, mid_ref, right_ref)):
        ref[:, :CELLS] = res_ref[side]
        ref[:, CELLS:] = charge
    for copy in zero_copies:
        copy.wait()


def add_kernel(kept_ref, left_ref, right_ref, dens_ref, head_ref, tail_ref):
    dens = kept_ref[:, :CELLS] + left_ref[:, :CELLS] + right_ref[:, :CELLS]
    dens_ref[...] = dens
    head_ref[...] = dens[:, :LAYER]
    tail_ref[:, :LAYER] = dens[:, CELLS - LAYER :]
    tail_ref[:, LAYER:] = kept_ref[:, CELLS:] + left_ref[:, CELLS:]


def potential_of(density, before, after, average):
    lane = lax.broadcasted_iota(jnp.int32, density.shape, 1)
    along_z = lane & (SIDE - 1)
    along_y = (lane // SIDE) & (SIDE - 1)
    scale = omega * four_pi / 6.0
    source = density - average
    one = scale * source
    padded = jnp.concatenate([scale * (before - average), one, scale * (after - average)], axis=1)
    beside = padded[:, :CELLS] + padded[:, 2 * LAYER :]

    def moved(steps):
        return pltpu.roll(one, steps % CELLS, 1)

    beside += jnp.where(along_y > 0, moved(SIDE), moved(SIDE - LAYER))
    beside += jnp.where(along_y < SIDE - 1, moved(-SIDE), moved(LAYER - SIDE))
    beside += jnp.where(along_z > 0, moved(1), moved(1 - SIDE))
    beside += jnp.where(along_z < SIDE - 1, moved(-1), moved(SIDE - 1))
    two = one + omega * ((four_pi * source + beside) / 6.0 - one)
    root = jnp.exp(jnp.log(jnp.abs(density)) * (1.0 / 3.0))
    return two - slater * jnp.where(density < 0.0, -root, root)


def ham_kernel(
    devices, bricks_ref, cx_ref, cy_ref, cz_ref, ex_ref,
    left_ref, mid_ref, right_ref, before_ref, after_ref, charge_ref, zeroed_ref,
    pot_ref, ham_ref,
    order_ref, count_ref, tables_ref, x_ref, y_ref, z_ref, orb_a, orb_b, v_ref, acc_ref, sum_ref, seen_ref,
    table_sem, ham_sems,
):
    fetch_tables(devices, (cx_ref, cy_ref, cz_ref, ex_ref), tables_ref, table_sem)
    list_blocks(devices, bricks_ref, order_ref, count_ref)

    def clear(at, carry):
        seen_ref[at] = 0
        return carry

    lax.fori_loop(0, BLK_DEV * COLS, clear, 0)

    def wide(ref):
        return jnp.broadcast_to(ref[:, :CELLS], (8, min(ref.shape[1], CELLS)))

    average = jnp.sum(charge_ref[...]) / (devices * CELLS)
    left, mid, right = wide(left_ref), wide(mid_ref), wide(right_ref)
    v_ref[0] = potential_of(left, wide(before_ref)[:, :LAYER], mid[:, :LAYER], average)
    own_potential = potential_of(mid, left[:, CELLS - LAYER :], right[:, :LAYER], average)
    v_ref[1] = own_potential
    v_ref[2] = potential_of(right, mid[:, CELLS - LAYER :], wide(after_ref)[:, :LAYER], average)
    pot_ref[...] = own_potential[:1]
    pltpu.make_async_copy(tables_ref, tables_ref, table_sem).wait()

    def await_rows(side, rows_half):
        pltpu.make_async_copy(
            sum_ref.at[pl.ds(0, PAIR), pl.ds(0, WIDE)], ham_ref.at[pl.ds(0, PAIR), pl.ds(0, WIDE)],
            ham_sems.at[side, rows_half],
        ).wait()

    def await_brick(side):
        lax.fori_loop(0, count_ref[side] // 2, lambda half, inner: (await_rows(side, half), inner)[1], 0)

    def one_brick(side, carry):
        factors(devices, side, order_ref, tables_ref, x_ref, y_ref, z_ref)

        def steps(rows):
            def step(t, inner):
                for part, orb_ref in ((0, orb_a), (1, orb_b)):
                    orbital_chunk(part, t, x_ref, y_ref, z_ref, orb_ref)
                    at = pl.ds(pl.multiple_of(t * 2 * CHUNK + part * CHUNK, CHUNK), CHUNK)
                    v = v_ref[side, pl.ds(0, 1), at]
                    mine = orb_ref[:, :rows].T
                    weighted = (mine.astype(jnp.float32) * v).astype(jnp.bfloat16)
                    acc_ref[:rows, :] += jnp.dot(weighted, orb_ref[...], preferred_element_type=jnp.float32)
                return inner

            acc_ref[:rows, :] = jnp.zeros((rows, WIDE), jnp.float32)
            lax.fori_loop(0, CELLS // (2 * CHUNK), step, 0)

        pl.when(count_ref[side] == 2)(lambda: steps(PAIR))
        pl.when(count_ref[side] != 2)(lambda: steps(2 * PAIR))
        pl.when(side > 0)(lambda: await_brick(jnp.maximum(side - 1, 0)))

        def put(at, inner):
            a, c = at // KB, lax.rem(at, KB)
            row, col = place(devices, order_ref, side, a, c)
            block = (aligned(row, FB), aligned(col, FB))
            piece = acc_ref[aligned(a, FB), aligned(c, FB)] * (64.0 / CELLS)
            seen = seen_ref[row * COLS + col]

            @pl.when(seen == 0)
            def _():
                sum_ref[block] = piece

            @pl.when(seen != 0)
            def _():
                sum_ref[block] += piece

            seen_ref[row * COLS + col] = 1
            pltpu.make_async_copy(sum_ref.at[block], ham_ref.at[block], ham_sems.at[side, a // 2]).start()
            return inner

        lax.fori_loop(0, count_ref[side] * KB, put, 0)
        return carry

    lax.fori_loop(0, 3, one_brick, 0)
    await_brick(2)


def f32(*shape):
    return jax.ShapeDtypeStruct(shape, jnp.float32)


def solution(mesh):
    devices = mesh.shape["dev"]

    def moved_by(value, steps):
        return lax.ppermute(value, "dev", [(i, (i + steps) % devices) for i in range(devices)])

    shared_scratch = [
        pltpu.SMEM((3 * KB,), jnp.int32),
        pltpu.SMEM((3,), jnp.int32),
        pltpu.VMEM((4, TILES * TILE, FB), jnp.float32),
        pltpu.VMEM((SIDE, WIDE), jnp.float32),
        pltpu.VMEM((SIDE, WIDE), jnp.float32),
        pltpu.VMEM((SIDE, WIDE), jnp.float32),
        pltpu.VMEM((CHUNK, WIDE), jnp.bfloat16),
        pltpu.VMEM((CHUNK, WIDE), jnp.bfloat16),
    ]

    def local(density_rows, center_x, center_y, center_z, exponent, brick_blocks):
        tables = [t.reshape(-1, FB) for t in (center_x, center_y, center_z, exponent)]
        bricks = brick_blocks.T
        to_left, kept, to_right, zeroed = pl.pallas_call(
            lambda *refs: density_kernel(devices, *refs),
            out_shape=[f32(1, CELLS + FB)] * 3 + [f32(BLK_DEV * FB, COLS * FB)],
            in_specs=[SMEM] + [HBM] * 5,
            out_specs=[VMEM] * 3 + [HBM],
            scratch_shapes=shared_scratch
            + [
                pltpu.VMEM((3, 2 * PAIR, WIDE), jnp.bfloat16),
                pltpu.VMEM((FB, COLS * FB), jnp.float32),
                pltpu.VMEM((3, 1, CELLS), jnp.float32),
                pltpu.SemaphoreType.DMA(()),
                pltpu.SemaphoreType.DMA((3, 2)),
                pltpu.SemaphoreType.DMA((BLK_DEV,)),
            ],
            compiler_params=pltpu.CompilerParams(vmem_limit_bytes=LIMIT),
        )(bricks, *tables, density_rows)
        from_right = moved_by(to_left, -1)
        from_left = moved_by(to_right, 1)
        density, head, tail = pl.pallas_call(
            add_kernel,
            out_shape=[f32(1, CELLS), f32(1, LAYER), f32(1, LAYER + FB)],
            in_specs=[VMEM] * 3,
            out_specs=[VMEM] * 3,
        )(kept, from_left, from_right)
        before = moved_by(tail, 2)
        left = moved_by(density, 1)
        right = moved_by(density, -1)
        after = moved_by(head, -2)
        charge = tail[:, LAYER:] + before[:, LAYER:]
        steps = 4
        while steps < devices:
            charge = charge + moved_by(charge, steps)
            steps *= 2
        return pl.pallas_call(
            lambda *refs: ham_kernel(devices, *refs),
            out_shape=[f32(1, CELLS), f32(BLK_DEV * FB, COLS * FB)],
            in_specs=[SMEM] + [HBM] * 4 + [VMEM] * 6 + [HBM],
            out_specs=[VMEM, HBM],
            scratch_shapes=shared_scratch
            + [
                pltpu.VMEM((3, 8, CELLS), jnp.float32),
                pltpu.VMEM((2 * PAIR, WIDE), jnp.float32),
                pltpu.VMEM((BLK_DEV * FB, COLS * FB), jnp.float32),
                pltpu.SMEM((BLK_DEV * COLS,), jnp.int32),
                pltpu.SemaphoreType.DMA(()),
                pltpu.SemaphoreType.DMA((3, 2)),
            ],
            input_output_aliases={11: 1},
            compiler_params=pltpu.CompilerParams(vmem_limit_bytes=LIMIT),
        )(bricks, *tables, left, density, right, before, after, charge, zeroed)

    return jax.shard_map(
        local,
        mesh=mesh,
        in_specs=(P("dev", None), P(), P(), P(), P(), P()),
        out_specs=(P("dev", None), P("dev", None)),
        check_vma=False,
    )
```

time: 120 us -> 106 us (0.88)
  Pallas kernels: 61.9 us -> 42.5 us
  waiting for transfers between devices: 24.3 us -> 36.6 us
  starting transfers between devices: 22.3 us -> 14.3 us
    ppermute x6 -> x11, waiting for transfers between devices: 1.45 us -> 36.6 us  [moved_by(): lax.ppermute(value, 'dev', [(i, (i + steps) % devices) for i in range(dev...]
    ppermute x7 -> x0, waiting for transfers between devices: 22.9 us -> none  [local(): lax.ppermute(charge, 'dev', [(i, i ^ steps) for i in range(devices)])]
    pallas_call x1, Pallas kernels: 27.9 us -> 17.2 us  [local(): pl.pallas_call(lambda *refs: density_kernel(devices, *refs), out_shape=[f...]
    pallas_call x1, Pallas kernels: 32.6 us -> 23.9 us  [local(): pl.pallas_call(lambda *refs: ham_kernel(devices, *refs), out_shape=[f32(1...]
    ppermute x6 -> x11, starting transfers between devices: 21.8 us -> 14.3 us  [moved_by(): lax.ppermute(value, 'dev', [(i, (i + steps) % devices) for i in range(dev...]
    unnamed x25 -> x28, local copies, waits for them, and re-layouts: 10.7 us -> 11.2 us
  transfers between devices with their start and end apart: 13 -> 11, of which waited for: 7 -> 7; matrix products, arithmetic and copies ran while one was open for 0% -> 1% of each run, Pallas kernels for 0% -> 0%
where the time goes in v2:
time: 106 us
  Pallas kernels  42.5 us (40%)
  waiting for transfers between devices  36.6 us (35%)
  starting transfers between devices  14.3 us (13%)
  local copies, waits for them, and re-layouts  11.2 us (11%)
    ppermute x11, waiting for transfers between devices, moved_by(): lax.ppermute(value, 'dev', [(i, (i + steps) % devices) for i in range(dev...  36.6 us
    pallas_call x1, Pallas kernels, local(): pl.pallas_call(lambda *refs: ham_kernel(devices, *refs), out_shape=[f32(1...  23.9 us
    pallas_call x1, Pallas kernels, local(): pl.pallas_call(lambda *refs: density_kernel(devices, *refs), out_shape=[f...  17.2 us
    ppermute x11, starting transfers between devices, moved_by(): lax.ppermute(value, 'dev', [(i, (i + steps) % devices) for i in range(dev...  14.3 us
    unnamed x28, local copies, waits for them, and re-layouts  11.2 us
  transfers between devices with their start and end apart: 11, of which 7 were waited for; matrix products, arithmetic and copies ran while one was open for 1% of the time, Pallas kernels for 0%

profile of v2, /device:TPU:0, one launch (start us, length us, event | category | flops | bytes accessed | tf_op | source)
XLA Modules:
  0.0 106.2 jit_solution(16804426248243376851)
XLA Ops:
  0.6 0.0 copy-start
  0.6 1.0 copy-done
  1.6 1.0 copy-done.2
  2.6 1.0 copy-done.4
  3.6 1.0 copy-done.6
  4.6 0.7 copy-done.10
  5.3 17.2 %shard_map.77 = (f32[1,4224]{1,0:T(1,128)S(1)}, f32[1,4224]{1,0:T(1,128)S(1)}, f32[1,4224]{1,0:T(1,128)S(1)}, f32[768,3840]{1,0:T(8,128)}) custom-call(s32[8,128]{1,0:T(8,128)S(1)} %bitcast.13, f32[768,128]{1,0:T(8,128)S(1)} %bitcast.5, f32[768,128]{1,0:T(8,128)S(1)} %bitcast.7, f32[768,128]{1,0:T(8,128)S(1)} %bitcast.9, f32[768,128]{1,0:T(8,128)S(1)} %bitcast.11, ...), custom_call_target="tpu_custom_call" | custom-call | tf_op jit(solution)/shard_map/pallas_call | solution.py:326
  22.5 0.6 copy-done.8
  23.1 0.0 collective-permute-start
  23.1 7.2 %collective-permute-start.1 = (f32[1,4224]{1,0:T(1,128)S(1)}, f32[1,4224]{1,0:T(1,128)S(1)}, u32[]{:S(2)}, u32[]{:S(2)}) collective-permute-start(f32[1,4224]{1,0:T(1,128)S(1)} %get-tuple-element.11), channel_id=1, source_target_pairs={{0,127},{1,0},{2,1},{3,2},{4,3},{5,4},{6,5},{7,6},{8,7},{9,8},{10,... | collective-permute-start | bytes 50696 | tf_op jit(solution)/shard_map/ppermute | solution.py:310
  30.3 1.4 %collective-permute-done.left_ref = f32[1,4224]{1,0:T(1,128)S(1)} collective-permute-done((f32[1,4224]{1,0:T(1,128)S(1)}, f32[1,4224]{1,0:T(1,128)S(1)}, u32[]{:S(2)}, u32[]{:S(2)}) %collective-permute-start) | collective-permute-done | bytes 16928 | tf_op jit(solution)/shard_map/ppermute | solution.py:310
  31.7 0.0 collective-permute-done.1.right_ref
  31.8 0.6 copy-done.12
  32.3 0.0 copy-done.13
  32.4 1.4 %shard_map.78 = (f32[1,4096]{1,0:T(1,128)}, f32[1,256]{1,0:T(1,128)}, f32[1,384]{1,0:T(1,128)}) custom-call(f32[1,4224]{1,0:T(1,128)} %copy-done.8, f32[1,4224]{1,0:T(1,128)} %copy-done.12, f32[1,4224]{1,0:T(1,128)} %copy-done.13), custom_call_target="tpu_custom_call" | custom-call | tf_op jit(solution)/shard_map/pallas_call | solution.py:344
  33.7 7.2 %collective-permute-start.3 = (f32[1,4096]{1,0:T(1,128)}, f32[1,4096]{1,0:T(1,128)S(1)}, u32[]{:S(2)}, u32[]{:S(2)}) collective-permute-start(f32[1,4096]{1,0:T(1,128)} %get-tuple-element.12.refs_6_), channel_id=1, source_target_pairs={{0,127},{1,0},{2,1},{3,2},{4,3},{5,4},{6,5},{7,6},{8,7},{9,8},{10,... | collective-permute-start | bytes 49160 | tf_op jit(solution)/shard_map/ppermute | solution.py:310
  40.9 2.1 %collective-permute-done.4.refs_8_ = f32[1,384]{1,0:T(1,128)S(1)} collective-permute-done((f32[1,384]{1,0:T(1,128)}, f32[1,384]{1,0:T(1,128)S(1)}, u32[]{:S(2)}, u32[]{:S(2)}) %collective-permute-start.4) | collective-permute-done | bytes 1568 | tf_op jit(solution)/shard_map/ppermute | solution.py:310
  42.9 0.7 slice_add_fusion
  43.6 9.3 %collective-permute-done.6 = f32[1,128]{1,0:T(1,128)S(1)} collective-permute-done((f32[1,128]{1,0:T(1,128)S(1)}, f32[1,128]{1,0:T(1,128)S(1)}, u32[]{:S(2)}, u32[]{:S(2)}) %collective-permute-start.6) | collective-permute-done | bytes 544 | tf_op jit(solution)/shard_map/ppermute | solution.py:310
  52.9 6.9 %collective-permute-done.7 = f32[1,128]{1,0:T(1,128)S(1)} collective-permute-done((f32[1,128]{1,0:T(1,128)S(1)}, f32[1,128]{1,0:T(1,128)S(1)}, u32[]{:S(2)}, u32[]{:S(2)}) %collective-permute-start.7) | collective-permute-done | bytes 544 | tf_op jit(solution)/shard_map/ppermute | solution.py:310
  59.8 7.2 %collective-permute-done.8 = f32[1,128]{1,0:T(1,128)S(1)} collective-permute-done((f32[1,128]{1,0:T(1,128)S(1)}, f32[1,128]{1,0:T(1,128)S(1)}, u32[]{:S(2)}, u32[]{:S(2)}) %collective-permute-start.8) | collective-permute-done | bytes 544 | tf_op jit(solution)/shard_map/ppermute | solution.py:310
  66.9 4.7 %collective-permute-done.9 = f32[1,128]{1,0:T(1,128)S(1)} collective-permute-done((f32[1,128]{1,0:T(1,128)S(1)}, f32[1,128]{1,0:T(1,128)S(1)}, u32[]{:S(2)}, u32[]{:S(2)}) %collective-permute-start.9) | collective-permute-done | bytes 544 | tf_op jit(solution)/shard_map/ppermute | solution.py:310
  71.7 0.0 collective-permute-start.10
  71.7 5.0 %collective-permute-done.10 = f32[1,128]{1,0:T(1,128)S(1)} collective-permute-done((f32[1,128]{1,0:T(1,128)S(1)}, f32[1,128]{1,0:T(1,128)S(1)}, u32[]{:S(2)}, u32[]{:S(2)}) %collective-permute-start.10) | collective-permute-done | bytes 544 | tf_op jit(solution)/shard_map/ppermute | solution.py:310
  76.7 0.0 copy-start.1
  76.8 1.0 copy-done.1
  77.7 1.0 copy-done.3
  78.7 1.0 copy-done.5
  79.7 1.0 copy-done.7
  80.7 0.7 copy-done.9
  81.4 0.7 copy-done.11
  82.1 23.9 %shard_map.79 = (f32[1,4096]{1,0:T(1,128)}, f32[768,3840]{1,0:T(8,128)}) custom-call(s32[8,128]{1,0:T(8,128)S(1)} %bitcast.14, f32[768,128]{1,0:T(8,128)S(1)} %bitcast.6, f32[768,128]{1,0:T(8,128)S(1)} %bitcast.8, f32[768,128]{1,0:T(8,128)S(1)} %bitcast.10, f32[768,128]{1,0:T(8,128)S(1)} %bitcast.12, ...), custom_call_target="tpu_custom_call", output_to_operand_aliasing={{1}: (11, {})} | custom-call | tf_op jit(solution)/shard_map/pallas_call | solution.py:359
  (27 shorter events, 0.1 us)
Async XLA Ops:
  0.6 1.0 copy-start
  1.6 1.0 copy-start.2
  2.6 1.0 copy-start.4
  3.6 1.0 copy-start.6
  4.6 0.7 copy-start.10
  22.5 0.6 copy-start.8
  23.1 8.6 %collective-permute-start = (f32[1,4224]{1,0:T(1,128)S(1)}, f32[1,4224]{1,0:T(1,128)S(1)}, u32[]{:S(2)}, u32[]{:S(2)}) collective-permute-start(f32[1,4224]{1,0:T(1,128)S(1)} %get-tuple-element.10), channel_id=1, source_target_pairs={{0,1},{1,2},{2,3},{3,4},{4,5},{5,6},{6,7},{7,8},{8,9},{9,10},{10,1... | collective-permute-start | bytes 50696 | tf_op jit(solution)/shard_map/ppermute | solution.py:310
  23.1 8.6 %collective-permute-start.1 = (f32[1,4224]{1,0:T(1,128)S(1)}, f32[1,4224]{1,0:T(1,128)S(1)}, u32[]{:S(2)}, u32[]{:S(2)}) collective-permute-start(f32[1,4224]{1,0:T(1,128)S(1)} %get-tuple-element.11), channel_id=1, source_target_pairs={{0,127},{1,0},{2,1},{3,2},{4,3},{5,4},{6,5},{7,6},{8,7},{9,8},{10,... | collective-permute-start | bytes 50696 | tf_op jit(solution)/shard_map/ppermute | solution.py:310
  31.7 0.6 copy-start.12
  31.8 0.6 copy-start.13
  33.7 9.2 %collective-permute-start.4 = (f32[1,384]{1,0:T(1,128)}, f32[1,384]{1,0:T(1,128)S(1)}, u32[]{:S(2)}, u32[]{:S(2)}) collective-permute-start(f32[1,384]{1,0:T(1,128)} %get-tuple-element.13), channel_id=1, source_target_pairs={{0,2},{1,3},{2,4},{3,5},{4,6},{5,7},{6,8},{7,9},{8,10},{9,11},{10,... | collective-permute-start | bytes 4616 | tf_op jit(solution)/shard_map/ppermute | solution.py:310
  33.7 43.0 %collective-permute-start.3 = (f32[1,4096]{1,0:T(1,128)}, f32[1,4096]{1,0:T(1,128)S(1)}, u32[]{:S(2)}, u32[]{:S(2)}) collective-permute-start(f32[1,4096]{1,0:T(1,128)} %get-tuple-element.12.refs_6_), channel_id=1, source_target_pairs={{0,127},{1,0},{2,1},{3,2},{4,3},{5,4},{6,5},{7,6},{8,7},{9,8},{10,... | collective-permute-start | bytes 49160 | tf_op jit(solution)/shard_map/ppermute | solution.py:310
  40.9 35.8 %collective-permute-start.2 = (f32[1,4096]{1,0:T(1,128)}, f32[1,4096]{1,0:T(1,128)S(1)}, u32[]{:S(2)}, u32[]{:S(2)}) collective-permute-start(f32[1,4096]{1,0:T(1,128)} %get-tuple-element.12.refs_6_), channel_id=1, source_target_pairs={{0,1},{1,2},{2,3},{3,4},{4,5},{5,6},{6,7},{7,8},{8,9},{9,10},{10,1... | collective-permute-start | bytes 49160 | tf_op jit(solution)/shard_map/ppermute | solution.py:310
  43.6 9.3 %collective-permute-start.6 = (f32[1,128]{1,0:T(1,128)S(1)}, f32[1,128]{1,0:T(1,128)S(1)}, u32[]{:S(2)}, u32[]{:S(2)}) collective-permute-start(f32[1,128]{1,0:T(1,128)S(1)} %slice_add_fusion), channel_id=1, source_target_pairs={{0,4},{1,5},{2,6},{3,7},{4,8},{5,9},{6,10},{7,11},{8,12},{9,13},{1... | collective-permute-start | bytes 1544 | tf_op jit(solution)/shard_map/ppermute | solution.py:310
  52.9 6.9 %collective-permute-start.7 = (f32[1,128]{1,0:T(1,128)S(1)}, f32[1,128]{1,0:T(1,128)S(1)}, u32[]{:S(2)}, u32[]{:S(2)}) collective-permute-start(f32[1,128]{1,0:T(1,128)S(1)} %add.19), channel_id=1, source_target_pairs={{0,8},{1,9},{2,10},{3,11},{4,12},{5,13},{6,14},{7,15},{8,16},{9,17... | collective-permute-start | bytes 1544 | tf_op jit(solution)/shard_map/ppermute | solution.py:310
  59.8 7.2 %collective-permute-start.8 = (f32[1,128]{1,0:T(1,128)S(1)}, f32[1,128]{1,0:T(1,128)S(1)}, u32[]{:S(2)}, u32[]{:S(2)}) collective-permute-start(f32[1,128]{1,0:T(1,128)S(1)} %add.20), channel_id=1, source_target_pairs={{0,16},{1,17},{2,18},{3,19},{4,20},{5,21},{6,22},{7,23},{8,24},{9,... | collective-permute-start | bytes 1544 | tf_op jit(solution)/shard_map/ppermute | solution.py:310
  66.9 4.8 %collective-permute-start.9 = (f32[1,128]{1,0:T(1,128)S(1)}, f32[1,128]{1,0:T(1,128)S(1)}, u32[]{:S(2)}, u32[]{:S(2)}) collective-permute-start(f32[1,128]{1,0:T(1,128)S(1)} %add.21), channel_id=1, source_target_pairs={{0,32},{1,33},{2,34},{3,35},{4,36},{5,37},{6,38},{7,39},{8,40},{9,... | collective-permute-start | bytes 1544 | tf_op jit(solution)/shard_map/ppermute | solution.py:310
  66.9 9.8 %collective-permute-start.5 = (f32[1,256]{1,0:T(1,128)}, f32[1,256]{1,0:T(1,128)S(1)}, u32[]{:S(2)}, u32[]{:S(2)}) collective-permute-start(f32[1,256]{1,0:T(1,128)} %get-tuple-element.14), channel_id=1, source_target_pairs={{0,126},{1,127},{2,0},{3,1},{4,2},{5,3},{6,4},{7,5},{8,6},{9,7},{1... | collective-permute-start | bytes 3080 | tf_op jit(solution)/shard_map/ppermute | solution.py:310
  71.7 5.0 %collective-permute-start.10 = (f32[1,128]{1,0:T(1,128)S(1)}, f32[1,128]{1,0:T(1,128)S(1)}, u32[]{:S(2)}, u32[]{:S(2)}) collective-permute-start(f32[1,128]{1,0:T(1,128)S(1)} %add.22), channel_id=1, source_target_pairs={{0,64},{1,65},{2,66},{3,67},{4,68},{5,69},{6,70},{7,71},{8,72},{9,... | collective-permute-start | bytes 1544 | tf_op jit(solution)/shard_map/ppermute | solution.py:310
  76.7 1.0 copy-start.1
  77.7 1.0 copy-start.3
  78.7 1.0 copy-start.5
  79.7 1.0 copy-start.7
  80.7 0.7 copy-start.9
  81.4 0.7 copy-start.11
